TPU v7x, 512 devices: a whole 4x4x16 slice. The times are simulated.
512 devices in a mesh: dp: 32 (over y, x, z_hi), fsdp: 16 (over z_lo, core).
Axes of the slice: x: 4, y: 4, z: 16 (z_hi: 2, z_lo: 8; z = z_hi * 8 + z_lo), core: 2. Of those that a mesh axis runs over, the one named last changes fastest.
Arguments:
- hidden: bfloat16 [65536, 8192], P('dp', 'fsdp'), may hold values from -6 to 6
- gain: float32 [8192], P('fsdp'), may hold values from 0.1 to 1.9
- head_weight: bfloat16 [200, 8192], P(None, 'fsdp'), may hold values from -0.0625 to 0.0625
- lengths: int32 [256], replicated, may hold values from 1 to 1024, 65536 in all
- battles: int32 [1024, 2], replicated, may hold values from 0 to 199, all different within a row
Outputs:
- mean_loss: float32 [], replicated
- coef_table: float32 [256, 200], replicated
- grad_hidden: bfloat16 [65536, 8192], P('dp', 'fsdp')
- grad_head: float32 [200, 8192], P(None, 'fsdp')
- grad_gain: float32 [8192], P('fsdp')
Inputs may be any that keep to these rules, and one draw needn't show every extreme that they name: The lengths sum to 65536; the longest prompt has exactly 1024 tokens. `battles`: the two models of a battle differ; the winner comes first; every model fights somewhere.
All inputs are finite; a program needn't handle non-finite values.
Results may differ from a plain program's by a relative error of at most 0.0059.
Values may be sent and summed in bfloat16 or wider, within the bound.
A program may use at most 64 MiB of HBM per device.

v0:
```python
import jax
import jax.numpy as jnp
from jax import lax
from jax.sharding import PartitionSpec as P

D = 8192


def member_mask(ends, lengths, first_row, row_count):
    positions = first_row + jnp.arange(row_count, dtype=jnp.int32)
    starts = ends - lengths
    inside = (positions[None, :] >= starts[:, None]) & (positions[None, :] < ends[:, None])
    return inside.astype(jnp.float32)


def row_prompts(ends, first_row, row_count):
    positions = first_row + jnp.arange(row_count, dtype=jnp.int32)
    return jnp.sum((positions[:, None] >= ends[None, :]).astype(jnp.int32), axis=1)


def pool_rows(members, exp_logits):
    return jnp.dot(
        members, exp_logits, precision=lax.Precision.HIGHEST, preferred_element_type=jnp.float32
    )


def battle_terms(pooled, lengths, battles):
    coef_table = jnp.log(pooled / lengths.astype(jnp.float32)[:, None])
    per_prompt = battles.shape[0] // lengths.shape[0]
    prompt_of = jnp.arange(battles.shape[0], dtype=jnp.int32) // per_prompt
    win_coef = coef_table[prompt_of, battles[:, 0]]
    lose_coef = coef_table[prompt_of, battles[:, 1]]
    margin = lose_coef - win_coef
    mean_loss = jnp.mean(jax.nn.softplus(margin))
    battle_slope = jax.nn.sigmoid(margin) / battles.shape[0]
    grad_coef = jnp.zeros_like(coef_table).at[prompt_of, battles[:, 1]].add(battle_slope)
    grad_coef = grad_coef.at[prompt_of, battles[:, 0]].add(-battle_slope)
    return (coef_table, mean_loss, grad_coef / pooled)


def on_device(hidden, gain, head_weight, lengths, battles):
    tok_rows = hidden.shape[0]
    hidden_f = hidden.astype(jnp.float32)
    square_total = lax.psum(jnp.sum(hidden_f * hidden_f, axis=1), "fsdp")
    inv_rms = lax.rsqrt(square_total / D + 1e-06)
    normed = (hidden_f * inv_rms[:, None] * gain[None, :]).astype(jnp.bfloat16)
    ends = jnp.cumsum(lengths)
    base_row = lax.axis_index("dp") * tok_rows
    contract = (((1,), (1,)), ((), ()))
    partial_logits = lax.dot_general(
        normed, head_weight, contract, preferred_element_type=jnp.float32
    )
    logits = lax.psum(partial_logits, "fsdp")
    members = member_mask(ends, lengths, base_row, tok_rows)
    owner_ids = row_prompts(ends, base_row, tok_rows)
    exp_logits = jnp.exp(logits)
    local_pool = pool_rows(members, exp_logits)
    pooled = lax.psum(local_pool, "dp")
    coef_table, mean_loss, grad_ratio = battle_terms(pooled, lengths, battles)
    spread_ratio = jnp.take(grad_ratio, owner_ids, axis=0)
    local_grad = (exp_logits * spread_ratio).astype(jnp.bfloat16)
    head_part = lax.dot_general(
        local_grad, normed, (((0,), (0,)), ((), ())), preferred_element_type=jnp.float32
    )
    grad_normed = jnp.dot(local_grad, head_weight, preferred_element_type=jnp.float32)
    norm_stat = lax.psum(jnp.sum(grad_normed * gain[None, :] * hidden_f, axis=1), "fsdp")
    grad_hidden = (
        gain[None, :] * inv_rms[:, None] * grad_normed
        - hidden_f * (inv_rms**3 * norm_stat / D)[:, None]
    )
    gain_part = jnp.sum(grad_normed * hidden_f * inv_rms[:, None], axis=0)
    grad_head, grad_gain = lax.psum((head_part, gain_part), "dp")
    return (mean_loss, coef_table, grad_hidden.astype(jnp.bfloat16), grad_head, grad_gain)


def solution(mesh):
    placed = (P("dp", "fsdp"), P("fsdp"), P(None, "fsdp"), P(), P())
    return jax.shard_map(
        on_device,
        mesh=mesh,
        in_specs=placed,
        out_specs=(P(), P(), P("dp", "fsdp"), P(None, "fsdp"), P("fsdp")),
        check_vma=False,
    )
```

profile of v0, /device:TPU:1, one launch (start us, length us, event | category | flops | bytes accessed | tf_op | source)
XLA Modules:
  0.0 1441.5 jit_solution(1171645198012722540)
XLA Ops:
  7.2 2.2 fusion
  9.5 51.8 %psum.42 = f32[2048]{0:T(1024)S(1)} all-reduce(f32[2048]{0:T(1024)S(1)} %fusion), channel_id=1, replica_groups=mesh['dp'=32,'fsdp'=16] {'fsdp'}, use_global_device_ids=true, to_apply=%region_3.4 | all-reduce | flops 2048 | bytes 16384 | tf_op jit(solution)/shard_map/psum | solution.py:44
  61.4 2.2 fusion.18
  63.7 0.3 reduce-window.9
  64.0 0.1 slice.15
  64.2 0.1 slice_reduce_fusion
  64.3 0.1 multiply_reduce_fusion
  64.4 0.1 and_reduce_fusion
  64.5 0.1 fusion.26
  64.6 0.6 convert_reduce_fusion
  65.3 203.2 %all-reduce.4.cloned.1.call-done = f32[2048,200]{0,1:T(8,128)} async-done(((f32[2048,200]{0,1:T(8,128)}), f32[2048,200]{0,1:T(8,128)}) %all-reduce.4.cloned.1.call-update) | async-done | bytes 1638416 | tf_op jit(solution)/shard_map/psum | solution.py:53
  268.5 3.7 fusion.8
  272.2 547.9 %all-reduce.6.cloned.1.call-done = f32[256,200]{0,1:T(8,128)} async-done(((f32[256,200]{0,1:T(8,128)}), f32[256,200]{0,1:T(8,128)}) %all-reduce.6.cloned.1.call-update) | async-done | bytes 204816 | tf_op jit(solution)/shard_map/psum | solution.py:58
  820.1 1.0 divide_log_fusion
  821.1 8.6 gather_fusion.1
  829.7 8.6 gather_fusion
  838.4 0.6 fusion.25
  839.0 5.9 scatter_custom_fusion
  845.0 6.1 scatter_fusion
  851.1 0.1 reshape.130
  851.2 0.1 copy.14
  851.3 6.6 gather_fusion.2
  858.0 1.7 copy.15
  859.7 2.4 multiply_convert_fusion
  862.1 0.2 copy-done.3
  862.3 1.5 fusion.16
  863.8 2.8 fusion.7
  866.6 141.8 %psum.47 = f32[512]{0:T(512)} all-reduce(f32[512]{0:T(512)S(1)} %get-tuple-element.5), channel_id=1, replica_groups=mesh['dp'=32,'fsdp'=16] {'dp'}, use_global_device_ids=true, to_apply=%region_14.15 | all-reduce | flops 512 | bytes 4096 | tf_op jit(solution)/shard_map/psum | solution.py:72
  1008.4 80.9 %psum.45 = f32[2048]{0:T(1024)S(1)} all-reduce(f32[2048]{0:T(1024)S(1)} %get-tuple-element.6), channel_id=1, replica_groups=mesh['dp'=32,'fsdp'=16] {'fsdp'}, use_global_device_ids=true, to_apply=%region_11.12 | all-reduce | flops 2048 | bytes 16384 | tf_op jit(solution)/shard_map/psum | solution.py:66
  1089.9 3.7 fusion.5
  1093.6 338.5 %all-reduce.8.cloned.1.call-done = f32[200,512]{1,0:T(8,128)} async-done(((f32[200,512]{1,0:T(8,128)}), f32[200,512]{1,0:T(8,128)}) %all-reduce.8.cloned.1.call-update) | async-done | bytes 409616 | tf_op jit(solution)/shard_map/psum | solution.py:72
  1432.1 1.8 copy.20
  (36 shorter events, 0.4 us)
Async XLA Ops:
  7.2 54.2 %copy-start = (bf16[200,512]{1,0:T(8,128)(2,1)S(1)}, bf16[200,512]{1,0:T(8,128)(2,1)}, u32[]{:S(2)}) copy-start(bf16[200,512]{1,0:T(8,128)(2,1)} %param.7) | copy-start | bytes 614404
  7.2 54.1 %copy-start.2 = (bf16[2048,512]{1,0:T(8,128)(2,1)S(1)}, bf16[2048,512]{1,0:T(8,128)(2,1)}, u32[]{:S(2)}) copy-start(bf16[2048,512]{1,0:T(8,128)(2,1)} %param.5) | copy-start | bytes 6291460
  7.2 54.1 %copy-start.7 = (f32[512]{0:T(512)S(1)}, f32[512]{0:T(512)}, u32[]{:S(2)}) copy-start(f32[512]{0:T(512)} %param.6) | copy-start | bytes 6148
  7.2 261.3 %all-reduce.4.cloned.1.call-start = ((), (), s32[]{:S(2)}) async-start(), calls=%async_computation | async-start | bytes 3276800 | tf_op jit(solution)/shard_map/psum | solution.py:53
  61.3 2.3 copy-start.6
  61.4 2.8 copy-start.5
  61.4 2.9 copy-start.9
  61.4 3.0 copy-start.8
  63.6 756.5 %all-reduce.6.cloned.1.call-start = ((), (), s32[]{:S(2)}) async-start(), calls=%async_computation.1 | async-start | bytes 409600 | tf_op jit(solution)/shard_map/psum | solution.py:58
  272.1 1159.9 %all-reduce.8.cloned.1.call-start = ((), (), s32[]{:S(2)}) async-start(), calls=%async_computation.2 | async-start | bytes 819200 | tf_op jit(solution)/shard_map/psum | solution.py:72
  821.1 8.7 copy-start.1
  845.0 6.2 copy-start.4
  859.7 2.6 copy-start.3
Sparse Core Ops, SparseCore 0:
  63.7 204.6 all-reduce.3
  272.3 547.7 all-reduce.5
  866.7 565.2 all-reduce.7
where the time goes:
time: 1460 us; the launch traced here: 1440 us
  waiting for transfers between devices  1090 us (75%)
  blocking collectives  274 us (19%)
  local copies, waits for them, and re-layouts  28.1 us (2%)
  other arithmetic  23.3 us (2%)
  between operations  15.8 us (1%)
    psum x1, waiting for transfers between devices, on_device(): pooled = lax.psum(local_pool, 'dp')  548 us
    psum x1, waiting for transfers between devices, on_device(): grad_head, grad_gain = lax.psum((head_part, gain_part), 'dp')  338 us
    psum x1, waiting for transfers between devices, on_device(): logits = lax.psum(partial_logits, 'fsdp')  203 us
    psum x1, blocking collectives, on_device(): grad_head, grad_gain = lax.psum((head_part, gain_part), 'dp')  142 us
    psum x1, blocking collectives, on_device(): lax.psum(jnp.sum(grad_normed * gain[None, :] * hidden_f, axis=1), 'fsdp')  80.9 us
    psum x1, blocking collectives, on_device(): square_total = lax.psum(jnp.sum(hidden_f * hidden_f, axis=1), 'fsdp')  51.8 us
  transfers between devices with their start and end apart: 3, of which 3 were waited for; matrix products, arithmetic and copies ran while one was open for 0% of the time, Pallas kernels for 0%

commit v1 on v0

v1 whole, which is shorter than its diff:
```python
import functools

import jax
import jax.numpy as jnp
from jax import lax
from jax.experimental import pallas as pl
from jax.experimental.pallas import tpu as pltpu
from jax.sharding import PartitionSpec as P

Y, X, ZH, ZL, NC = 4, 4, 2, 8, 2
XY, F, DP = Y * X, ZL * NC, Y * X * ZH
LANES = 128
PAIRS = 4
EPS = 1e-06
MESH = pl.DeviceIdType.MESH
F32, BF16 = jnp.float32, jnp.bfloat16


def nn(a, b):
    return lax.dot_general(a, b, (((1,), (0,)), ((), ())), preferred_element_type=F32)


def nt(a, b):
    return lax.dot_general(a, b, (((1,), (1,)), ((), ())), preferred_element_type=F32)


def tn(a, b):
    return lax.dot_general(a, b, (((0,), (0,)), ((), ())), preferred_element_type=F32)


def split3(x):
    hi = x.astype(BF16).astype(F32)
    mid = (x - hi).astype(BF16).astype(F32)
    return jnp.concatenate([hi, mid, x - hi - mid], axis=0).astype(BF16)


def join3(x):
    rows = x.shape[0] // 3
    return x[:rows] + x[rows : 2 * rows] + x[2 * rows :]


def kernel(
    models, width, n_battles, blk,
    hidden_hbm, gain_hbm, head_hbm, lens_hbm, battles_hbm,
    loss_ref, coef_ref, gh_hbm, ghead_ref, ggain_ref,
    hid, gain_v, head_v, lens_v, bat_v, wp, wpad, members, ids, raw16, out_v,
    s1_send, s1_recv, s2_buf, s3_send, s3_recv, g_t, g_tile, g_send, s4_recv,
    s5_send, s5_recv, ag, c1_recv, c2_send, c2_recv, c_blk, c5_all, c5_sum, c5_other, ctab,
    load_sem, out_sem, s1_ss, s1_rs, s2_ss, s2_rs, s3_ss, s3_rs, s4_ss, s4_rs, s5_ss, s5_rs,
    s6_ss, s6_rs, c1_ss, c1_rs, c2_ss, c2_rs, c5_ss, c5_rs, c5b_ss, c5b_rs, c6_ss, c6_rs,
):
    toks, dl = hid.shape
    prompts = members.shape[1]
    tiles = -(-models // 16)
    slots = c1_recv.shape[0]
    dp = lax.axis_index("dp")
    f = lax.axis_index("fsdp")
    xy, zh = dp // ZH, dp % ZH
    y, x = xy // X, xy % X
    zl, c = f // NC, f % NC
    base = dp * toks

    def fsdp_peer(k):
        return lax.rem(f + k, F)

    def xy_peer(k):
        return lax.rem(y + k // X, Y) * X + lax.rem(x + k % X, X)

    def xy_dev(q):
        return (q * ZH + zh, f)

    zh_dev = (xy * ZH + (1 - zh), f)
    dp_next = (lax.rem(dp + 1, DP), f)
    dp_prev = (lax.rem(dp + DP - 1, DP), f)

    loads = [
        pltpu.make_async_copy(lens_hbm, lens_v, load_sem.at[0]),
        pltpu.make_async_copy(battles_hbm, bat_v, load_sem.at[1]),
        pltpu.make_async_copy(gain_hbm, gain_v, load_sem.at[2]),
        pltpu.make_async_copy(head_hbm, head_v, load_sem.at[3]),
    ]
    n_blk = toks // blk
    for i in range(n_blk):
        rows = pl.ds(i * blk, blk)
        loads.append(pltpu.make_async_copy(hidden_hbm.at[rows], hid.at[rows], load_sem.at[4 + i]))
    for cp in loads:
        cp.start()

    barrier = pltpu.get_barrier_semaphore()
    partners = [(dp, fsdp_peer(k)) for k in range(1, F)]
    partners += [xy_dev(xy_peer(k)) for k in range(1, XY)]
    partners += [zh_dev, dp_next, dp_prev]
    for dev in partners:
        pl.semaphore_signal(barrier, inc=1, device_id=dev, device_id_type=MESH)

    loads[0].wait()
    lens = jnp.broadcast_to(lens_v[...], (8, prompts))
    len_hi = lens // 32
    len_lo = lens - len_hi * 32
    upto = (
        lax.broadcasted_iota(jnp.int32, (prompts, prompts), 0)
        <= lax.broadcasted_iota(jnp.int32, (prompts, prompts), 1)
    ).astype(F32).astype(BF16)
    ends = (32.0 * nn(len_hi.astype(F32).astype(BF16), upto) + nn(len_lo.astype(F32).astype(BF16), upto))[:1]
    ends = ends.astype(jnp.int32)
    lens = lens[:1]
    starts = ends - lens
    lens_f = lens.astype(F32)
    at_prev = ((starts < base) & (ends > base)).astype(F32)
    at_next = ((starts < base + toks) & (ends > base + toks)).astype(F32)
    owned = ((ends > base) & (ends <= base + toks)).astype(F32)
    for i in range(n_blk):
        pos = base + i * blk + lax.broadcasted_iota(jnp.int32, (blk, prompts), 0)
        inside = (pos >= starts) & (pos < ends)
        members[pl.ds(i * blk, blk), :] = inside.astype(F32).astype(BF16)
    loads[1].wait()
    ids[...] = nt(bat_v[...].astype(F32).astype(BF16), members[...])

    loads[2].wait()
    loads[3].wait()
    wide = 16 * tiles
    head_f = head_v[...].astype(F32)
    if wide > models:
        head_f = jnp.concatenate([head_f, jnp.zeros((wide - models, dl), F32)], axis=0)
    wpad[...] = head_f.astype(BF16)
    wp[...] = (head_f * gain_v[...]).astype(BF16)

    model_of = lax.broadcasted_iota(jnp.int32, (wide, LANES), 0).astype(F32)
    ones_l = jnp.ones((8, LANES), BF16)
    for t in range(tiles, slots * NC):
        raw16[t // NC, t % NC] = jnp.zeros((16, toks), BF16)
    for i in range(n_blk):
        loads[4 + i].wait()
        rows = pl.ds(i * blk, blk)
        h = hid[rows, :]
        raw = nt(wp[...], h)
        for t in range(tiles):
            raw16[t // NC, t % NC, :, rows] = raw[16 * t : 16 * t + 16].astype(BF16)
        hf = h.astype(F32)
        sq = hf * hf
        part = sq[:, :LANES]
        for j in range(1, dl // LANES):
            part = part + sq[:, j * LANES : (j + 1) * LANES]
        part_hi = part.astype(BF16)
        part_lo = (part - part_hi.astype(F32)).astype(BF16)
        sumsq = nt(ones_l, part_hi) + nt(ones_l, part_lo)
        for b in range(blk // LANES):
            lanes = slice(b * LANES, (b + 1) * LANES)
            dest = i * (blk // LANES) + b
            block = raw[:, lanes]
            id_blk = ids[:, pl.ds(i * blk + b * LANES, LANES)]
            picked = [
                jnp.sum(jnp.where(model_of == id_blk[j : j + 1], block, 0.0), axis=0, keepdims=True)
                for j in range(2 * PAIRS)
            ]
            s1_send[dest, 0:8, :] = jnp.concatenate(picked, axis=0)
            s1_send[dest, 8:16, :] = sumsq[:, lanes]

    pl.semaphore_wait(barrier, len(partners))

    def remote(src, dst, ss, rs, dev):
        cp = pltpu.make_async_remote_copy(
            src_ref=src, dst_ref=dst, send_sem=ss, recv_sem=rs, device_id=dev, device_id_type=MESH
        )
        cp.start()
        return cp

    s1 = [
        remote(s1_send.at[fsdp_peer(k)], s1_recv.at[k], s1_ss.at[k], s1_rs.at[k], (dp, fsdp_peer(k)))
        for k in range(1, F)
    ]
    c1 = remote(raw16.at[:, 1 - c], c1_recv, c1_ss, c1_rs, (dp, zl * NC + (1 - c)))
    c1.wait()
    for i in range(slots):
        c2_send[i] = (raw16[i, c].astype(F32) + c1_recv[i].astype(F32)).astype(BF16)

    for cp in s1:
        cp.wait_recv()
    acc = s1_send[f]
    for k in range(1, F):
        acc = acc + s1_recv[k]
    inv = lax.rsqrt(acc[8:16] / width + EPS)
    s2_buf[f] = jnp.concatenate([acc[0:8] * inv, inv], axis=0)
    s2 = [
        remote(s2_buf.at[f], s2_buf.at[f], s2_ss.at[k], s2_rs.at[k], (dp, fsdp_peer(k)))
        for k in range(1, F)
    ]

    def c2_copy(k):
        to = lax.rem(zl + k, ZL)
        return to, pltpu.make_async_remote_copy(
            src_ref=c2_send.at[lax.rem(to, slots)], dst_ref=c2_recv.at[k], send_sem=c2_ss.at[k],
            recv_sem=c2_rs.at[k], device_id=(dp, to * NC + c), device_id_type=MESH,
        )

    for k in range(1, ZL):
        to, cp = c2_copy(k)

        @pl.when(to < slots)
        def _():
            cp.start()

    for cp in s2:
        cp.wait_recv()
    logits = jnp.concatenate([s2_buf[r, 0:8, :] for r in range(F)], axis=1)
    inv = jnp.concatenate([s2_buf[r, 8:16, :] for r in range(F)], axis=1)
    exps = jnp.exp(logits)
    pooled = join3(nn(split3(exps), members[...]))

    s3_send[0] = jnp.broadcast_to(jnp.sum(pooled * at_next, axis=1, keepdims=True), (8, LANES))
    s3_send[1] = jnp.broadcast_to(jnp.sum(pooled * at_prev, axis=1, keepdims=True), (8, LANES))
    s3 = [
        remote(s3_send.at[0], s3_recv.at[0], s3_ss.at[0], s3_rs.at[0], dp_next),
        remote(s3_send.at[1], s3_recv.at[1], s3_ss.at[1], s3_rs.at[1], dp_prev),
    ]
    for cp in s3:
        cp.wait_recv()
    spread = [1] * (prompts // LANES)
    from_prev = jnp.concatenate([s3_recv[0] for _ in spread], axis=1)
    from_next = jnp.concatenate([s3_recv[1] for _ in spread], axis=1)
    pooled = pooled + from_prev * at_prev + from_next * at_next
    pooled = jnp.where(pooled > 0.0, pooled, 1.0)
    coef = jnp.log(pooled / lens_f)
    other = jnp.concatenate([coef[PAIRS:], coef[:PAIRS]], axis=0)
    row_of = lax.broadcasted_iota(jnp.int32, (8, prompts), 0)
    sign = jnp.where(row_of < PAIRS, -1.0, 1.0)
    margin = sign * (coef - other)
    softplus = jnp.maximum(margin, 0.0) + jnp.log1p(jnp.exp(-jnp.abs(margin)))
    loss_part = jnp.sum(jnp.where(row_of < PAIRS, softplus * owned, 0.0)) / n_battles
    ratio = sign * (1.0 / (1.0 + jnp.exp(-margin))) / n_battles / pooled
    grads = exps * join3(nt(split3(ratio), members[...]))
    slope = jnp.sum(grads * logits, axis=0, keepdims=True) * inv[:1] * inv[:1] / width
    grads = grads * inv

    for b in range(toks // LANES):
        lanes = slice(b * LANES, (b + 1) * LANES)
        id_blk = ids[:, lanes]
        full = jnp.zeros((wide, LANES), F32)
        for j in range(2 * PAIRS):
            full = full + jnp.where(model_of == id_blk[j : j + 1], grads[j : j + 1, lanes], 0.0)
        g_t[:, lanes] = full.astype(BF16)
    head_part = nn(g_t[...], hid[...])
    for t in range(tiles):
        g_tile[t] = head_part[16 * t : 16 * t + 16]
        g_send[t] = head_part[16 * t : 16 * t + 16].astype(BF16)
    for t in range(tiles, XY):
        g_tile[t] = jnp.zeros((16, dl), F32)
        g_send[t] = jnp.zeros((16, dl), BF16)
    s4 = [
        remote(g_send.at[xy_peer(k)], s4_recv.at[k], s4_ss.at[k], s4_rs.at[k], xy_dev(xy_peer(k)))
        for k in range(1, XY)
    ]

    for k in range(1, ZL):
        to, cp = c2_copy(k)

        @pl.when(zl < slots)
        def _():
            cp.wait_recv()

    c_blk[...] = jnp.zeros((16, prompts), F32)

    @pl.when(zl < slots)
    def _():
        total = c2_send[zl].astype(F32)
        for k in range(1, ZL):
            total = total + c2_recv[k].astype(F32)
        c_blk[...] = join3(nn(split3(jnp.exp(total * inv[:1])), members[...]))

    mine = jnp.where(f == tiles, loss_part, c_blk[...])
    c5_all[xy] = mine
    c5 = [
        remote(c5_all.at[xy], c5_all.at[xy], c5_ss.at[k], c5_rs.at[k], xy_dev(xy_peer(k)))
        for k in range(1, XY)
    ]

    c_rows = lax.broadcasted_iota(jnp.int32, (16, toks), 0)
    slope_hi = slope.astype(BF16).astype(F32)
    slope_lo = slope - slope_hi
    slope3 = jnp.where(c_rows == 0, slope_hi, jnp.where(c_rows == 1, slope_lo, 0.0)).astype(BF16)
    ones_w = jnp.ones((16, dl), BF16)
    outs = []
    for i in range(n_blk):
        rows = pl.ds(i * blk, blk)
        gn = tn(g_t[:, rows], wpad[...])
        cb = tn(slope3[:, i * blk : (i + 1) * blk], ones_w)
        out_v[rows, :] = (gain_v[...] * gn - hid[rows, :].astype(F32) * cb).astype(BF16)
        cp = pltpu.make_async_copy(out_v.at[rows], gh_hbm.at[rows], out_sem.at[i])
        cp.start()
        outs.append(cp)

    for cp in s4:
        cp.wait_recv()
    total = g_tile[xy]
    for k in range(1, XY):
        total = total + s4_recv[k].astype(F32)
    s5_send[...] = total
    s5 = remote(s5_send, s5_recv, s5_ss, s5_rs, zh_dev)

    for cp in c5:
        cp.wait_recv()
    csum = c5_all[0]
    for q in range(1, XY):
        csum = csum + c5_all[q]
    c5_sum[...] = csum
    c5b = remote(c5_sum, c5_other, c5b_ss, c5b_rs, zh_dev)

    s5.wait_recv()
    ag[xy] = (s5_send[...] + s5_recv[...]).astype(BF16)
    s6 = [
        remote(ag.at[xy], ag.at[xy], s6_ss.at[k], s6_rs.at[k], xy_dev(xy_peer(k)))
        for k in range(1, XY)
    ]

    c5b.wait_recv()
    csum = c5_sum[...] + c5_other[...]
    loss_hi = csum.astype(BF16).astype(F32)
    crow = lax.broadcasted_iota(jnp.int32, (16, prompts), 0)
    loss_blk = jnp.where(crow == 0, loss_hi, jnp.where(crow == 1, csum - loss_hi, 0.0))
    coef_blk = jnp.log(csum / lens_f)
    ctab[f] = jnp.where(f == tiles, loss_blk, coef_blk).astype(BF16)
    c6 = [
        remote(ctab.at[f], ctab.at[f], c6_ss.at[k], c6_rs.at[k], (dp, fsdp_peer(k)))
        for k in range(1, F)
    ]

    for cp in s6:
        cp.wait_recv()
    whole = jnp.concatenate([ag[t].astype(F32) for t in range(tiles)], axis=0)
    ghead_ref[...] = (gain_v[...] * whole)[:models]
    ggain_ref[...] = jnp.sum(wpad[...].astype(F32) * whole, axis=0, keepdims=True)

    for cp in c6:
        cp.wait_recv()
    table = jnp.concatenate([ctab[t].astype(F32) for t in range(tiles)], axis=0)
    coef_ref[...] = jnp.transpose(table)[:, :models]
    loss_ref[0, 0] = jnp.sum(ctab[tiles].astype(F32)[0:2, 0:1])

    for cp in s1 + [c for c in s2] + s3 + s4 + [s5] + s6 + c5 + [c5b] + c6:
        cp.wait_send()
    for k in range(1, ZL):
        to, cp = c2_copy(k)

        @pl.when(to < slots)
        def _():
            cp.wait_send()

    for cp in outs:
        cp.wait()


def on_device(hidden, gain, head_weight, lengths, battles):
    toks, dl = hidden.shape
    models = head_weight.shape[0]
    prompts = lengths.shape[0]
    n_battles = battles.shape[0]
    tiles = -(-models // 16)
    wide = 16 * tiles
    slots = -(-tiles // NC)
    blk = min(512, toks)
    sem = pltpu.SemaphoreType.DMA
    rows8 = battles.reshape(prompts, PAIRS, 2).transpose(2, 1, 0).reshape(2 * PAIRS, prompts)
    vmem = pl.BlockSpec(memory_space=pltpu.VMEM)
    smem = pl.BlockSpec(memory_space=pltpu.SMEM)
    hbm = pl.BlockSpec(memory_space=pl.ANY)
    V = pltpu.VMEM
    loss, coef, gh, ghead, ggain = pl.pallas_call(
        functools.partial(kernel, models, float(dl * F), float(n_battles), blk),
        out_shape=(
            jax.ShapeDtypeStruct((1, 1), F32),
            jax.ShapeDtypeStruct((prompts, models), F32),
            jax.ShapeDtypeStruct((toks, dl), BF16),
            jax.ShapeDtypeStruct((models, dl), F32),
            jax.ShapeDtypeStruct((1, dl), F32),
        ),
        in_specs=[hbm] * 5,
        out_specs=(smem, vmem, hbm, vmem, vmem),
        scratch_shapes=[
            V((toks, dl), BF16), V((1, dl), F32), V((models, dl), BF16),
            V((1, prompts), jnp.int32), V((2 * PAIRS, prompts), jnp.int32),
            V((wide, dl), BF16), V((wide, dl), BF16),
            V((toks, prompts), BF16), V((2 * PAIRS, toks), F32),
            V((slots, NC, 16, toks), BF16), V((toks, dl), BF16),
            V((F, 16, LANES), F32), V((F, 16, LANES), F32), V((F, 16, LANES), F32),
            V((2, 8, LANES), F32), V((2, 8, LANES), F32),
            V((wide, toks), BF16), V((XY, 16, dl), F32), V((XY, 16, dl), BF16),
            V((XY, 16, dl), BF16), V((16, dl), F32), V((16, dl), F32), V((XY, 16, dl), BF16),
            V((slots, 16, toks), BF16), V((slots, 16, toks), BF16), V((ZL, 16, toks), BF16),
            V((16, prompts), F32), V((XY, 16, prompts), F32), V((16, prompts), F32),
            V((16, prompts), F32), V((F, 16, prompts), BF16),
            sem((4 + toks // blk,)), sem((toks // blk,)),
            sem((F,)), sem((F,)), sem((F,)), sem((F,)), sem((2,)), sem((2,)),
            sem((XY,)), sem((XY,)), sem, sem, sem((XY,)), sem((XY,)),
            sem, sem, sem((ZL,)), sem((ZL,)), sem((XY,)), sem((XY,)), sem, sem,
            sem((F,)), sem((F,)),
        ],
        compiler_params=pltpu.CompilerParams(
            collective_id=0, has_side_effects=True, vmem_limit_bytes=48 * 2**20
        ),
        name="head",
    )(hidden, gain.reshape(1, dl), head_weight, lengths.reshape(1, prompts), rows8)
    return loss.reshape(()), coef, gh, ghead, ggain.reshape(dl)


def solution(mesh):
    placed = (P("dp", "fsdp"), P("fsdp"), P(None, "fsdp"), P(), P())
    return jax.shard_map(
        on_device,
        mesh=mesh,
        in_specs=placed,
        out_specs=(P(), P(), P("dp", "fsdp"), P(None, "fsdp"), P("fsdp")),
        check_vma=False,
    )
```

time: 1460 us -> 99.4 us (0.07); the launches traced: 1440 us -> 99.1 us
  waiting for transfers between devices: 1090 us -> 0 us
  blocking collectives: 274 us -> 0 us
  Pallas kernels: 0 us -> 88.2 us
  other arithmetic: 23.3 us -> 0 us
  local copies, waits for them, and re-layouts: 28.1 us -> 8.42 us
    psum x3 -> x0, waiting for transfers between devices: 1090 us -> none  [the longest x1 548 us: on_device(): pooled = lax.psum(local_pool, 'dp')]
    psum x3 -> x0, blocking collectives: 274 us -> none  [the longest x1 142 us: on_device(): grad_head, grad_gain = lax.psum((head_part, gain_part), 'dp')]
    pallas_call x0 -> x1, Pallas kernels: none -> 88.2 us  [on_device(): pl.pallas_call(functools.partial(kernel, models, float(dl * F), float(n_b...]
    gather x4 -> x0, local copies, waits for them, and re-layouts: 25.6 us -> none  [the longest x1 8.65 us: battle_terms(): lose_coef = coef_table[prompt_of, battles[:, 1]]]
  transfers between devices with their start and end apart: 3 -> 0, of which waited for: 3 -> 0; matrix products, arithmetic and copies ran while one was open for 0% -> 0% of each run, Pallas kernels for 0% -> 0%
where the time goes in v1:
time: 99.4 us; the launch traced here: 99.1 us
  Pallas kernels  88.2 us (89%)
  local copies, waits for them, and re-layouts  8.42 us (8%)
  between operations  2.41 us (2%)
    pallas_call x1, Pallas kernels, on_device(): pl.pallas_call(functools.partial(kernel, models, float(dl * F), float(n_b...  88.2 us
    unnamed x12, local copies, waits for them, and re-layouts  7.34 us

profile of v1, /device:TPU:1, one launch (start us, length us, event | category | flops | bytes accessed | tf_op | source)
XLA Modules:
  0.0 99.1 jit_solution(8511466076510903837)
XLA Ops:
  0.6 1.0 reshape.30
  1.6 0.1 copy.12
  1.7 0.0 copy-start
  1.7 1.6 %copy-done = bf16[2048,512]{1,0:T(8,128)(2,1)S(1)} copy-done((bf16[2048,512]{1,0:T(8,128)(2,1)S(1)}, bf16[2048,512]{1,0:T(8,128)(2,1)}, u32[]{:S(2)}) %copy-start) | copy-done | bytes 2097176
  3.3 0.0 copy-start.1
  3.3 0.9 copy-done.1
  4.3 0.0 copy-start.2
  4.3 0.7 copy-done.2
  4.9 0.0 copy-start.3
  4.9 0.7 copy-done.3
  5.6 88.2 %head.1 = (f32[1,1]{1,0:T(1,128)}, f32[256,200]{1,0:T(8,128)S(1)}, bf16[2048,512]{1,0:T(8,128)(2,1)S(1)}, f32[200,512]{1,0:T(8,128)S(1)}, f32[1,512]{1,0:T(1,128)S(1)}) custom-call(bf16[2048,512]{1,0:T(8,128)(2,1)S(1)} %copy-done, f32[1,512]{1,0:T(1,128)S(1)} %bitcast.7, bf16[200,512]{1,0:T(8,128)(2,1)S(1)} %copy-done.1, s32[1,256]{1,0:T(1,128)S(1)} %bitcast.9, ...), custom_call_target="tpu_custom_call" | custom-call | tf_op jit(solution)/shard_map/head/pallas_call | solution.py:367
  93.9 0.8 copy.13
  95.3 1.3 %copy.19 = bf16[2048,512]{1,0:T(8,128)(2,1)} copy(bf16[2048,512]{1,0:T(8,128)(2,1)S(1)} %get-tuple-element.32) | data formatting | bytes 4194304
  96.6 0.8 copy.20
  97.4 0.6 copy.21
  (1 shorter events, 0.0 us)
Async XLA Ops:
  1.7 1.6 %copy-start = (bf16[2048,512]{1,0:T(8,128)(2,1)S(1)}, bf16[2048,512]{1,0:T(8,128)(2,1)}, u32[]{:S(2)}) copy-start(bf16[2048,512]{1,0:T(8,128)(2,1)} %hidden_hbm.1) | copy-start | bytes 6291460
  3.3 0.9 copy-start.1
  4.3 0.7 copy-start.2
  4.9 0.7 copy-start.3

commit v2 on v1

--- a/solution.py
+++ b/solution.py
@@ -44,15 +44,16 @@
     hidden_hbm, gain_hbm, head_hbm, lens_hbm, battles_hbm,
     loss_ref, coef_ref, gh_hbm, ghead_ref, ggain_ref,
     hid, gain_v, head_v, lens_v, bat_v, wp, wpad, members, ids, raw16, out_v,
-    s1_send, s1_recv, s2_buf, s3_send, s3_recv, g_t, g_tile, g_send, s4_recv,
-    s5_send, s5_recv, ag, c1_recv, c2_send, c2_recv, c_blk, c5_all, c5_sum, c5_other, ctab,
-    load_sem, out_sem, s1_ss, s1_rs, s2_ss, s2_rs, s3_ss, s3_rs, s4_ss, s4_rs, s5_ss, s5_rs,
-    s6_ss, s6_rs, c1_ss, c1_rs, c2_ss, c2_rs, c5_ss, c5_rs, c5b_ss, c5b_rs, c6_ss, c6_rs,
+    q_send, q_recv, i_buf, s1_send, s1_recv, s2_buf, s3_send, s3_recv, g_t, g_tile, g_send, s4_recv,
+    s5_send, s5_recv, ag, c1_recv, c5_all, c5_sum, c5_other, ctab,
+    load_sem, out_sem, q_ss, q_rs, i_ss, i_rs, s1_ss, s1_rs, s2_ss, s2_rs, s3_ss, s3_rs, s4_ss, s4_rs,
+    s5_ss, s5_rs, s6_ss, s6_rs, c1_ss, c1_rs, c2_ss, c2_rs, c5_ss, c5_rs, c5b_ss, c5b_rs, c6_ss, c6_rs, *halves,
 ):
     toks, dl = hid.shape
     prompts = members.shape[1]
     tiles = -(-models // 16)
-    slots = c1_recv.shape[0]
+    levels = len(halves) // 2
+    half, half_recv = halves[:levels], halves[levels:]
     dp = lax.axis_index("dp")
     f = lax.axis_index("fsdp")
     xy, zh = dp // ZH, dp % ZH
@@ -114,7 +115,15 @@
         inside = (pos >= starts) & (pos < ends)
         members[pl.ds(i * blk, blk), :] = inside.astype(F32).astype(BF16)
     loads[1].wait()
-    ids[...] = nt(bat_v[...].astype(F32).astype(BF16), members[...])
+    n_bat = bat_v.shape[1]
+    bat_row = lax.broadcasted_iota(jnp.int32, (2 * PAIRS, n_bat), 0)
+    bat_lane = lax.broadcasted_iota(jnp.int32, (2 * PAIRS, n_bat), 1)
+    bat = jnp.where(bat_row < PAIRS, bat_v[0:1, :], bat_v[1:2, :])
+    bat = jnp.where(bat_lane % PAIRS == bat_row % PAIRS, bat, 0)
+    judged = lax.broadcasted_iota(jnp.int32, (n_bat, prompts), 0) // PAIRS
+    judged = judged == lax.broadcasted_iota(jnp.int32, (n_bat, prompts), 1)
+    bat = nn(bat.astype(F32).astype(BF16), judged.astype(F32).astype(BF16))
+    ids[...] = nt(bat.astype(BF16), members[...])
 
     loads[2].wait()
     loads[3].wait()
@@ -125,18 +134,17 @@
     wpad[...] = head_f.astype(BF16)
     wp[...] = (head_f * gain_v[...]).astype(BF16)
 
-    model_of = lax.broadcasted_iota(jnp.int32, (wide, LANES), 0).astype(F32)
+    def remote(src, dst, ss, rs, dev):
+        cp = pltpu.make_async_remote_copy(
+            src_ref=src, dst_ref=dst, send_sem=ss, recv_sem=rs, device_id=dev, device_id_type=MESH
+        )
+        cp.start()
+        return cp
+
     ones_l = jnp.ones((8, LANES), BF16)
-    for t in range(tiles, slots * NC):
-        raw16[t // NC, t % NC] = jnp.zeros((16, toks), BF16)
     for i in range(n_blk):
         loads[4 + i].wait()
-        rows = pl.ds(i * blk, blk)
-        h = hid[rows, :]
-        raw = nt(wp[...], h)
-        for t in range(tiles):
-            raw16[t // NC, t % NC, :, rows] = raw[16 * t : 16 * t + 16].astype(BF16)
-        hf = h.astype(F32)
+        hf = hid[pl.ds(i * blk, blk), :].astype(F32)
         sq = hf * hf
         part = sq[:, :LANES]
         for j in range(1, dl // LANES):
@@ -145,65 +153,84 @@
         part_lo = (part - part_hi.astype(F32)).astype(BF16)
         sumsq = nt(ones_l, part_hi) + nt(ones_l, part_lo)
         for b in range(blk // LANES):
+            q_send[i * (blk // LANES) + b] = sumsq[0:1, b * LANES : (b + 1) * LANES]
+    pl.semaphore_wait(barrier, len(partners))
+    q_cp = [
+        remote(q_send.at[fsdp_peer(k)], q_recv.at[k], q_ss.at[k], q_rs.at[k], (dp, fsdp_peer(k)))
+        for k in range(1, F)
+    ]
+
+    model_of = lax.broadcasted_iota(jnp.int32, (wide, LANES), 0).astype(F32)
+    for t in range(tiles, ZL * NC):
+        raw16[t // NC, t % NC] = jnp.zeros((16, toks), BF16)
+    for i in range(n_blk):
+        rows = pl.ds(i * blk, blk)
+        raw = nt(wp[...], hid[rows, :])
+        for t in range(tiles):
+            raw16[t // NC, t % NC, :, rows] = raw[16 * t : 16 * t + 16].astype(BF16)
+        for b in range(blk // LANES):
             lanes = slice(b * LANES, (b + 1) * LANES)
-            dest = i * (blk // LANES) + b
             block = raw[:, lanes]
             id_blk = ids[:, pl.ds(i * blk + b * LANES, LANES)]
             picked = [
                 jnp.sum(jnp.where(model_of == id_blk[j : j + 1], block, 0.0), axis=0, keepdims=True)
                 for j in range(2 * PAIRS)
             ]
-            s1_send[dest, 0:8, :] = jnp.concatenate(picked, axis=0)
-            s1_send[dest, 8:16, :] = sumsq[:, lanes]
-
-    pl.semaphore_wait(barrier, len(partners))
-
-    def remote(src, dst, ss, rs, dev):
-        cp = pltpu.make_async_remote_copy(
-            src_ref=src, dst_ref=dst, send_sem=ss, recv_sem=rs, device_id=dev, device_id_type=MESH
-        )
-        cp.start()
-        return cp
+            s1_send[i * (blk // LANES) + b] = jnp.concatenate(picked, axis=0)
 
     s1 = [
         remote(s1_send.at[fsdp_peer(k)], s1_recv.at[k], s1_ss.at[k], s1_rs.at[k], (dp, fsdp_peer(k)))
         for k in range(1, F)
     ]
     c1 = remote(raw16.at[:, 1 - c], c1_recv, c1_ss, c1_rs, (dp, zl * NC + (1 - c)))
-    c1.wait()
-    for i in range(slots):
-        c2_send[i] = (raw16[i, c].astype(F32) + c1_recv[i].astype(F32)).astype(BF16)
+    for cp in q_cp:
+        cp.wait_recv()
+    acc = q_send[f]
+    for k in range(1, F):
+        acc = acc + q_recv[k]
+    inv_own = lax.rsqrt(acc / width + EPS)
+    i_buf[f] = inv_own
+    i_cp = [
+        remote(i_buf.at[f], i_buf.at[f], i_ss.at[k], i_rs.at[k], (dp, fsdp_peer(k)))
+        for k in range(1, F)
+    ]
+
+    bits = [(zl >> n) % 2 for n in range(levels)]
+
+    def halve(n):
+        step = 1 << n
+        peer = (zl + step - 2 * step * bits[n]) * NC + c
+        return remote(half[n].at[:, 1 - bits[n]], half_recv[n], c2_ss.at[n], c2_rs.at[n], (dp, peer))
+
+    def fold(n):
+        for j in range(half_recv[n].shape[0]):
+            total = half[n][j, bits[n]].astype(F32) + half_recv[n][j].astype(F32)
+            half[n + 1][j // 2, j % 2] = total.astype(BF16)
+
+    c1.wait_recv()
+    for k in range(ZL):
+        half[0][k // 2, k % 2] = (raw16[k, c].astype(F32) + c1_recv[k].astype(F32)).astype(BF16)
+    c2 = [halve(0)]
 
     for cp in s1:
         cp.wait_recv()
     acc = s1_send[f]
     for k in range(1, F):
         acc = acc + s1_recv[k]
-    inv = lax.rsqrt(acc[8:16] / width + EPS)
-    s2_buf[f] = jnp.concatenate([acc[0:8] * inv, inv], axis=0)
+    s2_buf[f] = acc * inv_own
     s2 = [
         remote(s2_buf.at[f], s2_buf.at[f], s2_ss.at[k], s2_rs.at[k], (dp, fsdp_peer(k)))
         for k in range(1, F)
     ]
-
-    def c2_copy(k):
-        to = lax.rem(zl + k, ZL)
-        return to, pltpu.make_async_remote_copy(
-            src_ref=c2_send.at[lax.rem(to, slots)], dst_ref=c2_recv.at[k], send_sem=c2_ss.at[k],
-            recv_sem=c2_rs.at[k], device_id=(dp, to * NC + c), device_id_type=MESH,
-        )
-
-    for k in range(1, ZL):
-        to, cp = c2_copy(k)
-
-        @pl.when(to < slots)
-        def _():
-            cp.start()
-
-    for cp in s2:
-        cp.wait_recv()
-    logits = jnp.concatenate([s2_buf[r, 0:8, :] for r in range(F)], axis=1)
-    inv = jnp.concatenate([s2_buf[r, 8:16, :] for r in range(F)], axis=1)
+    for n in range(0, levels - 1)[:1]:
+        c2[n].wait_recv()
+        fold(n)
+        c2.append(halve(n + 1))
+
+    for cp in i_cp + s2:
+        cp.wait_recv()
+    logits = jnp.concatenate([s2_buf[r] for r in range(F)], axis=1)
+    inv = jnp.concatenate([i_buf[r] for r in range(F)], axis=1)
     exps = jnp.exp(logits)
     pooled = join3(nn(split3(exps), members[...]))
 
@@ -213,6 +240,10 @@
         remote(s3_send.at[0], s3_recv.at[0], s3_ss.at[0], s3_rs.at[0], dp_next),
         remote(s3_send.at[1], s3_recv.at[1], s3_ss.at[1], s3_rs.at[1], dp_prev),
     ]
+    for n in range(0, levels - 1)[1:]:
+        c2[n].wait_recv()
+        fold(n)
+        c2.append(halve(n + 1))
     for cp in s3:
         cp.wait_recv()
     spread = [1] * (prompts // LANES)
@@ -229,7 +260,7 @@
     loss_part = jnp.sum(jnp.where(row_of < PAIRS, softplus * owned, 0.0)) / n_battles
     ratio = sign * (1.0 / (1.0 + jnp.exp(-margin))) / n_battles / pooled
     grads = exps * join3(nt(split3(ratio), members[...]))
-    slope = jnp.sum(grads * logits, axis=0, keepdims=True) * inv[:1] * inv[:1] / width
+    slope = jnp.sum(grads * logits, axis=0, keepdims=True) * inv * inv / width
     grads = grads * inv
 
     for b in range(toks // LANES):
@@ -251,23 +282,10 @@
         for k in range(1, XY)
     ]
 
-    for k in range(1, ZL):
-        to, cp = c2_copy(k)
-
-        @pl.when(zl < slots)
-        def _():
-            cp.wait_recv()
-
-    c_blk[...] = jnp.zeros((16, prompts), F32)
-
-    @pl.when(zl < slots)
-    def _():
-        total = c2_send[zl].astype(F32)
-        for k in range(1, ZL):
-            total = total + c2_recv[k].astype(F32)
-        c_blk[...] = join3(nn(split3(jnp.exp(total * inv[:1])), members[...]))
-
-    mine = jnp.where(f == tiles, loss_part, c_blk[...])
+    c2[-1].wait_recv()
+    tile = half[-1][0, bits[-1]].astype(F32) + half_recv[-1][0].astype(F32)
+    c_blk = join3(nn(split3(jnp.exp(tile * inv)), members[...]))
+    mine = jnp.where(f == tiles, loss_part, c_blk)
     c5_all[xy] = mine
     c5 = [
         remote(c5_all.at[xy], c5_all.at[xy], c5_ss.at[k], c5_rs.at[k], xy_dev(xy_peer(k)))
@@ -333,19 +351,24 @@
     for cp in c6:
         cp.wait_recv()
     table = jnp.concatenate([ctab[t].astype(F32) for t in range(tiles)], axis=0)
-    coef_ref[...] = jnp.transpose(table)[:, :models]
+    coef_ref[...] = table[:models]
     loss_ref[0, 0] = jnp.sum(ctab[tiles].astype(F32)[0:2, 0:1])
 
-    for cp in s1 + [c for c in s2] + s3 + s4 + [s5] + s6 + c5 + [c5b] + c6:
+    for cp in q_cp + i_cp + s1 + s2 + s3 + s4 + [s5] + s6 + [c1] + c2 + c5 + [c5b] + c6:
         cp.wait_send()
-    for k in range(1, ZL):
-        to, cp = c2_copy(k)
-
-        @pl.when(to < slots)
-        def _():
-            cp.wait_send()
-
     for cp in outs:
+        cp.wait()
+
+
+def hand_out(loss, coef, gh, ghead, ggain, loss_o, coef_o, gh_o, ghead_o, ggain_o, sems):
+    rows = gh.shape[0] // 4
+    pairs = [(gh.at[pl.ds(n * rows, rows)], gh_o.at[pl.ds(n * rows, rows)]) for n in range(4)]
+    pairs += [(ghead, ghead_o), (coef, coef_o), (ggain, ggain_o)]
+    cps = [pltpu.make_async_copy(a, b, sems.at[n]) for n, (a, b) in enumerate(pairs)]
+    for cp in cps:
+        cp.start()
+    loss_o[0, 0] = loss[0, 0]
+    for cp in cps:
         cp.wait()
 
 
@@ -356,50 +379,63 @@
     n_battles = battles.shape[0]
     tiles = -(-models // 16)
     wide = 16 * tiles
-    slots = -(-tiles // NC)
     blk = min(512, toks)
+    levels = ZL.bit_length() - 1
     sem = pltpu.SemaphoreType.DMA
-    rows8 = battles.reshape(prompts, PAIRS, 2).transpose(2, 1, 0).reshape(2 * PAIRS, prompts)
     vmem = pl.BlockSpec(memory_space=pltpu.VMEM)
     smem = pl.BlockSpec(memory_space=pltpu.SMEM)
     hbm = pl.BlockSpec(memory_space=pl.ANY)
     V = pltpu.VMEM
-    loss, coef, gh, ghead, ggain = pl.pallas_call(
+    shapes = (
+        jax.ShapeDtypeStruct((1, 1), F32),
+        jax.ShapeDtypeStruct((models, prompts), F32),
+        jax.ShapeDtypeStruct((toks, dl), BF16),
+        jax.ShapeDtypeStruct((models, dl), F32),
+        jax.ShapeDtypeStruct((1, dl), F32),
+    )
+    results = pl.pallas_call(
         functools.partial(kernel, models, float(dl * F), float(n_battles), blk),
-        out_shape=(
-            jax.ShapeDtypeStruct((1, 1), F32),
-            jax.ShapeDtypeStruct((prompts, models), F32),
-            jax.ShapeDtypeStruct((toks, dl), BF16),
-            jax.ShapeDtypeStruct((models, dl), F32),
-            jax.ShapeDtypeStruct((1, dl), F32),
-        ),
+        out_shape=shapes,
         in_specs=[hbm] * 5,
         out_specs=(smem, vmem, hbm, vmem, vmem),
         scratch_shapes=[
             V((toks, dl), BF16), V((1, dl), F32), V((models, dl), BF16),
-            V((1, prompts), jnp.int32), V((2 * PAIRS, prompts), jnp.int32),
+            V((1, prompts), jnp.int32), V((2, n_battles), jnp.int32),
             V((wide, dl), BF16), V((wide, dl), BF16),
             V((toks, prompts), BF16), V((2 * PAIRS, toks), F32),
-            V((slots, NC, 16, toks), BF16), V((toks, dl), BF16),
-            V((F, 16, LANES), F32), V((F, 16, LANES), F32), V((F, 16, LANES), F32),
+            V((ZL, NC, 16, toks), BF16), V((toks, dl), BF16),
+            V((F, 1, LANES), F32), V((F, 1, LANES), F32), V((F, 1, LANES), F32),
+            V((F, 8, LANES), F32), V((F, 8, LANES), F32), V((F, 8, LANES), F32),
             V((2, 8, LANES), F32), V((2, 8, LANES), F32),
             V((wide, toks), BF16), V((XY, 16, dl), F32), V((XY, 16, dl), BF16),
             V((XY, 16, dl), BF16), V((16, dl), F32), V((16, dl), F32), V((XY, 16, dl), BF16),
-            V((slots, 16, toks), BF16), V((slots, 16, toks), BF16), V((ZL, 16, toks), BF16),
-            V((16, prompts), F32), V((XY, 16, prompts), F32), V((16, prompts), F32),
-            V((16, prompts), F32), V((F, 16, prompts), BF16),
+            V((ZL, 16, toks), BF16),
+            V((XY, 16, prompts), F32), V((16, prompts), F32), V((16, prompts), F32),
+            V((F, 16, prompts), BF16),
             sem((4 + toks // blk,)), sem((toks // blk,)),
+            sem((F,)), sem((F,)), sem((F,)), sem((F,)),
             sem((F,)), sem((F,)), sem((F,)), sem((F,)), sem((2,)), sem((2,)),
             sem((XY,)), sem((XY,)), sem, sem, sem((XY,)), sem((XY,)),
-            sem, sem, sem((ZL,)), sem((ZL,)), sem((XY,)), sem((XY,)), sem, sem,
+            sem, sem, sem((levels,)), sem((levels,)), sem((XY,)), sem((XY,)), sem, sem,
             sem((F,)), sem((F,)),
-        ],
+        ]
+        + [V((ZL >> (n + 1), 2, 16, toks), BF16) for n in range(levels)]
+        + [V((ZL >> (n + 1), 16, toks), BF16) for n in range(levels)],
         compiler_params=pltpu.CompilerParams(
-            collective_id=0, has_side_effects=True, vmem_limit_bytes=48 * 2**20
+            collective_id=0, has_side_effects=True, vmem_limit_bytes=60 * 2**20
         ),
         name="head",
-    )(hidden, gain.reshape(1, dl), head_weight, lengths.reshape(1, prompts), rows8)
-    return loss.reshape(()), coef, gh, ghead, ggain.reshape(dl)
+    )(hidden, gain.reshape(1, dl), head_weight, lengths.reshape(1, prompts), battles.T)
+    loss, coef, gh, ghead, ggain = pl.pallas_call(
+        hand_out,
+        out_shape=shapes,
+        in_specs=[smem] + [hbm] * 4,
+        out_specs=(smem,) + (hbm,) * 4,
+        scratch_shapes=[sem((7,))],
+        compiler_params=pltpu.CompilerParams(vmem_limit_bytes=60 * 2**20),
+        name="hand_out",
+    )(*results)
+    return loss.reshape(()), coef.T, gh, ghead, ggain.reshape(dl)
 
 
 def solution(mesh):

time: 99.4 us -> 160 us (1.61)
  Pallas kernels: 88.2 us -> 160 us
  local copies, waits for them, and re-layouts: 8.42 us -> 0 us
  between operations: 2.41 us -> 0.64 us
    pallas_call x0 -> x1, Pallas kernels: none -> 84.5 us  [on_device(): pl.pallas_call(hand_out, out_shape=shapes, in_specs=[smem] + [hbm] * 4, o...]
    pallas_call x1, Pallas kernels: 88.2 us -> 75.1 us  [on_device(): pl.pallas_call(functools.partial(kernel, models, float(dl * F), float(n_b...]
    unnamed x12 -> x0, local copies, waits for them, and re-layouts: 7.34 us -> none
where the time goes in v2:
time: 160 us
  Pallas kernels  160 us (100%)
    pallas_call x1, Pallas kernels, on_device(): pl.pallas_call(hand_out, out_shape=shapes, in_specs=[smem] + [hbm] * 4, o...  84.5 us
    pallas_call x1, Pallas kernels, on_device(): pl.pallas_call(functools.partial(kernel, models, float(dl * F), float(n_b...  75.1 us

profile of v2, /device:TPU:1, one launch (start us, length us, event | category | flops | bytes accessed | tf_op | source)
XLA Modules:
  0.0 160.2 jit_solution(1463091105404377258)
XLA Ops:
  0.6 75.1 %head.1 = (f32[1,1]{1,0:T(1,128)}, f32[200,256]{1,0:T(8,128)}, bf16[2048,512]{1,0:T(8,128)(2,1)}, f32[200,512]{1,0:T(8,128)}, f32[1,512]{1,0:T(1,128)}) custom-call(bf16[2048,512]{1,0:T(8,128)(2,1)} %hidden_hbm.1, f32[1,512]{1,0:T(1,128)} %bitcast.7, bf16[200,512]{1,0:T(8,128)(2,1)} %head_hbm.1, s32[1,256]{1,0:T(1,128)} %bitcast.8, s32[2,1024]{1,0:T(2,128)} %bitcast.6), custom_call_target="tpu_custom_call" | custom-call | tf_op jit(solution)/shard_map/head/pallas_call | solution.py:396
  75.8 84.5 %hand_out.1 = (f32[1,1]{1,0:T(1,128)}, f32[200,256]{1,0:T(8,128)}, bf16[2048,512]{1,0:T(8,128)(2,1)}, f32[200,512]{1,0:T(8,128)}, f32[1,512]{1,0:T(1,128)}) custom-call(f32[1,1]{1,0:T(1,128)} %get-tuple-element.15.loss, f32[200,256]{1,0:T(8,128)} %get-tuple-element.16.coef, bf16[2048,512]{1,0:T(8,128)(2,1)} %get-tuple-element.17.gh, ...), custom_call_target="tpu_custom_call" | custom-call | tf_op jit(solution)/shard_map/hand_out/pallas_call | solution.py:429

commit v3 on v2

--- a/solution.py
+++ b/solution.py
@@ -43,10 +43,10 @@
     models, width, n_battles, blk,
     hidden_hbm, gain_hbm, head_hbm, lens_hbm, battles_hbm,
     loss_ref, coef_ref, gh_hbm, ghead_ref, ggain_ref,
-    hid, gain_v, head_v, lens_v, bat_v, wp, wpad, members, ids, raw16, out_v,
-    q_send, q_recv, i_buf, s1_send, s1_recv, s2_buf, s3_send, s3_recv, g_t, g_tile, g_send, s4_recv,
+    hid, gain_v, head_v, lens_v, bat_v, wp, wpad, members, ids, raw, raw16, out_v,
+    q_send, q_recv, i_buf, s1_send, s1_recv, s2_buf, b_send, b_recv, g_t, g_tile, g_send, s4_recv,
     s5_send, s5_recv, ag, c1_recv, c5_all, c5_sum, c5_other, ctab,
-    load_sem, out_sem, q_ss, q_rs, i_ss, i_rs, s1_ss, s1_rs, s2_ss, s2_rs, s3_ss, s3_rs, s4_ss, s4_rs,
+    load_sem, out_sem, q_ss, q_rs, i_ss, i_rs, s1_ss, s1_rs, s2_ss, s2_rs, b_ss, b_rs, s4_ss, s4_rs,
     s5_ss, s5_rs, s6_ss, s6_rs, c1_ss, c1_rs, c2_ss, c2_rs, c5_ss, c5_rs, c5b_ss, c5b_rs, c6_ss, c6_rs, *halves,
 ):
     toks, dl = hid.shape
@@ -71,8 +71,7 @@
         return (q * ZH + zh, f)
 
     zh_dev = (xy * ZH + (1 - zh), f)
-    dp_next = (lax.rem(dp + 1, DP), f)
-    dp_prev = (lax.rem(dp + DP - 1, DP), f)
+    dp_next, dp_prev = lax.rem(dp + 1, DP), lax.rem(dp + DP - 1, DP)
 
     loads = [
         pltpu.make_async_copy(lens_hbm, lens_v, load_sem.at[0]),
@@ -90,7 +89,8 @@
     barrier = pltpu.get_barrier_semaphore()
     partners = [(dp, fsdp_peer(k)) for k in range(1, F)]
     partners += [xy_dev(xy_peer(k)) for k in range(1, XY)]
-    partners += [zh_dev, dp_next, dp_prev]
+    partners += [zh_dev]
+    partners += [(dp_prev if r >= F // 2 else dp_next, r) for r in range(F)]
     for dev in partners:
         pl.semaphore_signal(barrier, inc=1, device_id=dev, device_id_type=MESH)
 
@@ -110,6 +110,73 @@
     at_prev = ((starts < base) & (ends > base)).astype(F32)
     at_next = ((starts < base + toks) & (ends > base + toks)).astype(F32)
     owned = ((ends > base) & (ends <= base + toks)).astype(F32)
+    before_end = jnp.sum(at_prev * ends.astype(F32), axis=1, keepdims=True)
+    from_start = jnp.sum(at_next * starts.astype(F32), axis=1, keepdims=True)
+    from_start = jnp.where(jnp.sum(at_next, axis=1, keepdims=True) > 0.0, from_start, 2.0**30)
+
+    loads[2].wait()
+    loads[3].wait()
+    wide = 16 * tiles
+    head_f = head_v[...].astype(F32)
+    if wide > models:
+        head_f = jnp.concatenate([head_f, jnp.zeros((wide - models, dl), F32)], axis=0)
+    wpad[...] = head_f.astype(BF16)
+    wp[...] = (head_f * gain_v[...]).astype(BF16)
+
+    def remote(src, dst, ss, rs, dev):
+        cp = pltpu.make_async_remote_copy(
+            src_ref=src, dst_ref=dst, send_sem=ss, recv_sem=rs, device_id=dev, device_id_type=MESH
+        )
+        cp.start()
+        return cp
+
+    for t in range(tiles, ZL * NC):
+        raw16[t // NC, t % NC] = jnp.zeros((16, toks), BF16)
+    for i in range(n_blk):
+        loads[4 + i].wait()
+        rows = pl.ds(i * blk, blk)
+        block = nt(wp[...], hid[rows, :])
+        raw[:, rows] = block
+        for t in range(tiles):
+            raw16[t // NC, t % NC, :, rows] = block[16 * t : 16 * t + 16].astype(BF16)
+
+    pl.semaphore_wait(barrier, len(partners))
+    c1 = remote(raw16.at[:, 1 - c], c1_recv, c1_ss, c1_rs, (dp, zl * NC + (1 - c)))
+
+    ones_l = jnp.ones((8, LANES), BF16)
+    for i in range(n_blk):
+        hf = hid[pl.ds(i * blk, blk), :].astype(F32)
+        sq = hf * hf
+        part = sq[:, :LANES]
+        for j in range(1, dl // LANES):
+            part = part + sq[:, j * LANES : (j + 1) * LANES]
+        part_hi = part.astype(BF16)
+        part_lo = (part - part_hi.astype(F32)).astype(BF16)
+        sumsq = nt(ones_l, part_hi) + nt(ones_l, part_lo)
+        for b in range(blk // LANES):
+            q_send[i * (blk // LANES) + b] = sumsq[0:1, b * LANES : (b + 1) * LANES]
+    q_cp = [
+        remote(q_send.at[fsdp_peer(k)], q_recv.at[k], q_ss.at[k], q_rs.at[k], (dp, fsdp_peer(k)))
+        for k in range(1, F)
+    ]
+
+    bits = [(zl >> n) % 2 for n in range(levels)]
+
+    def halve(n):
+        step = 1 << n
+        peer = (zl + step - 2 * step * bits[n]) * NC + c
+        return remote(half[n].at[:, 1 - bits[n]], half_recv[n], c2_ss.at[n], c2_rs.at[n], (dp, peer))
+
+    def fold(n):
+        for j in range(half_recv[n].shape[0]):
+            total = half[n][j, bits[n]].astype(F32) + half_recv[n][j].astype(F32)
+            half[n + 1][j // 2, j % 2] = total.astype(BF16)
+
+    c1.wait_recv()
+    for k in range(ZL):
+        half[0][k // 2, k % 2] = (raw16[k, c].astype(F32) + c1_recv[k].astype(F32)).astype(BF16)
+    c2 = [halve(0)]
+
     for i in range(n_blk):
         pos = base + i * blk + lax.broadcasted_iota(jnp.int32, (blk, prompts), 0)
         inside = (pos >= starts) & (pos < ends)
@@ -125,64 +192,21 @@
     bat = nn(bat.astype(F32).astype(BF16), judged.astype(F32).astype(BF16))
     ids[...] = nt(bat.astype(BF16), members[...])
 
-    loads[2].wait()
-    loads[3].wait()
-    wide = 16 * tiles
-    head_f = head_v[...].astype(F32)
-    if wide > models:
-        head_f = jnp.concatenate([head_f, jnp.zeros((wide - models, dl), F32)], axis=0)
-    wpad[...] = head_f.astype(BF16)
-    wp[...] = (head_f * gain_v[...]).astype(BF16)
-
-    def remote(src, dst, ss, rs, dev):
-        cp = pltpu.make_async_remote_copy(
-            src_ref=src, dst_ref=dst, send_sem=ss, recv_sem=rs, device_id=dev, device_id_type=MESH
-        )
-        cp.start()
-        return cp
-
-    ones_l = jnp.ones((8, LANES), BF16)
-    for i in range(n_blk):
-        loads[4 + i].wait()
-        hf = hid[pl.ds(i * blk, blk), :].astype(F32)
-        sq = hf * hf
-        part = sq[:, :LANES]
-        for j in range(1, dl // LANES):
-            part = part + sq[:, j * LANES : (j + 1) * LANES]
-        part_hi = part.astype(BF16)
-        part_lo = (part - part_hi.astype(F32)).astype(BF16)
-        sumsq = nt(ones_l, part_hi) + nt(ones_l, part_lo)
-        for b in range(blk // LANES):
-            q_send[i * (blk // LANES) + b] = sumsq[0:1, b * LANES : (b + 1) * LANES]
-    pl.semaphore_wait(barrier, len(partners))
-    q_cp = [
-        remote(q_send.at[fsdp_peer(k)], q_recv.at[k], q_ss.at[k], q_rs.at[k], (dp, fsdp_peer(k)))
-        for k in range(1, F)
-    ]
-
     model_of = lax.broadcasted_iota(jnp.int32, (wide, LANES), 0).astype(F32)
-    for t in range(tiles, ZL * NC):
-        raw16[t // NC, t % NC] = jnp.zeros((16, toks), BF16)
-    for i in range(n_blk):
-        rows = pl.ds(i * blk, blk)
-        raw = nt(wp[...], hid[rows, :])
-        for t in range(tiles):
-            raw16[t // NC, t % NC, :, rows] = raw[16 * t : 16 * t + 16].astype(BF16)
-        for b in range(blk // LANES):
-            lanes = slice(b * LANES, (b + 1) * LANES)
-            block = raw[:, lanes]
-            id_blk = ids[:, pl.ds(i * blk + b * LANES, LANES)]
-            picked = [
-                jnp.sum(jnp.where(model_of == id_blk[j : j + 1], block, 0.0), axis=0, keepdims=True)
-                for j in range(2 * PAIRS)
-            ]
-            s1_send[i * (blk // LANES) + b] = jnp.concatenate(picked, axis=0)
+    for b in range(toks // LANES):
+        lanes = slice(b * LANES, (b + 1) * LANES)
+        block = raw[:, lanes]
+        id_blk = ids[:, lanes]
+        picked = [
+            jnp.sum(jnp.where(model_of == id_blk[j : j + 1], block, 0.0), axis=0, keepdims=True)
+            for j in range(2 * PAIRS)
+        ]
+        s1_send[b] = jnp.concatenate(picked, axis=0)
 
     s1 = [
         remote(s1_send.at[fsdp_peer(k)], s1_recv.at[k], s1_ss.at[k], s1_rs.at[k], (dp, fsdp_peer(k)))
         for k in range(1, F)
     ]
-    c1 = remote(raw16.at[:, 1 - c], c1_recv, c1_ss, c1_rs, (dp, zl * NC + (1 - c)))
     for cp in q_cp:
         cp.wait_recv()
     acc = q_send[f]
@@ -195,37 +219,39 @@
         for k in range(1, F)
     ]
 
-    bits = [(zl >> n) % 2 for n in range(levels)]
-
-    def halve(n):
-        step = 1 << n
-        peer = (zl + step - 2 * step * bits[n]) * NC + c
-        return remote(half[n].at[:, 1 - bits[n]], half_recv[n], c2_ss.at[n], c2_rs.at[n], (dp, peer))
-
-    def fold(n):
-        for j in range(half_recv[n].shape[0]):
-            total = half[n][j, bits[n]].astype(F32) + half_recv[n][j].astype(F32)
-            half[n + 1][j // 2, j % 2] = total.astype(BF16)
-
-    c1.wait_recv()
-    for k in range(ZL):
-        half[0][k // 2, k % 2] = (raw16[k, c].astype(F32) + c1_recv[k].astype(F32)).astype(BF16)
-    c2 = [halve(0)]
-
     for cp in s1:
         cp.wait_recv()
     acc = s1_send[f]
     for k in range(1, F):
         acc = acc + s1_recv[k]
-    s2_buf[f] = acc * inv_own
+    own = acc * inv_own
+    s2_buf[f] = own
     s2 = [
         remote(s2_buf.at[f], s2_buf.at[f], s2_ss.at[k], s2_rs.at[k], (dp, fsdp_peer(k)))
         for k in range(1, F)
     ]
-    for n in range(0, levels - 1)[:1]:
-        c2[n].wait_recv()
-        fold(n)
-        c2.append(halve(n + 1))
+    late = f >= F // 2
+    pos = base + f * LANES + lax.broadcasted_iota(jnp.int32, (8, LANES), 1)
+    pos = pos.astype(F32)
+    crossing = jnp.where(late, (pos >= from_start).astype(F32), (pos < before_end).astype(F32))
+    column = jnp.sum(jnp.exp(own) * crossing, axis=1, keepdims=True)
+    eye = lax.broadcasted_iota(jnp.int32, (8, LANES), 0) == lax.broadcasted_iota(jnp.int32, (8, LANES), 1)
+    b_send[...] = jnp.sum(jnp.where(eye, column, 0.0), axis=0, keepdims=True)
+    to_dp = jnp.where(late, dp_next, dp_prev)
+    b_cp = [
+        remote(b_send, b_recv.at[f], b_ss.at[k], b_rs.at[f], (to_dp, lax.rem(f + k, F)))
+        for k in range(F)
+    ]
+
+    def b_arrival(r):
+        return pltpu.make_async_remote_copy(
+            src_ref=b_send, dst_ref=b_recv.at[r], send_sem=b_ss.at[r], recv_sem=b_rs.at[r],
+            device_id=(to_dp, f), device_id_type=MESH,
+        )
+
+    c2[0].wait_recv()
+    fold(0)
+    c2.append(halve(1))
 
     for cp in i_cp + s2:
         cp.wait_recv()
@@ -233,24 +259,23 @@
     inv = jnp.concatenate([i_buf[r] for r in range(F)], axis=1)
     exps = jnp.exp(logits)
     pooled = join3(nn(split3(exps), members[...]))
-
-    s3_send[0] = jnp.broadcast_to(jnp.sum(pooled * at_next, axis=1, keepdims=True), (8, LANES))
-    s3_send[1] = jnp.broadcast_to(jnp.sum(pooled * at_prev, axis=1, keepdims=True), (8, LANES))
-    s3 = [
-        remote(s3_send.at[0], s3_recv.at[0], s3_ss.at[0], s3_rs.at[0], dp_next),
-        remote(s3_send.at[1], s3_recv.at[1], s3_ss.at[1], s3_rs.at[1], dp_prev),
-    ]
-    for n in range(0, levels - 1)[1:]:
+    for r in range(F):
+        b_arrival(r).wait_recv()
+
+    def column_of(rs):
+        row = b_recv[rs[0]]
+        for r in rs[1:]:
+            row = row + b_recv[r]
+        return jnp.sum(jnp.where(eye, row, 0.0), axis=1, keepdims=True)
+
+    from_prev = column_of(range(F // 2, F))
+    from_next = column_of(range(F // 2))
+    pooled = pooled + from_prev * at_prev + from_next * at_next
+    pooled = jnp.where(pooled > 0.0, pooled, 1.0)
+    for n in range(1, levels - 1):
         c2[n].wait_recv()
         fold(n)
         c2.append(halve(n + 1))
-    for cp in s3:
-        cp.wait_recv()
-    spread = [1] * (prompts // LANES)
-    from_prev = jnp.concatenate([s3_recv[0] for _ in spread], axis=1)
-    from_next = jnp.concatenate([s3_recv[1] for _ in spread], axis=1)
-    pooled = pooled + from_prev * at_prev + from_next * at_next
-    pooled = jnp.where(pooled > 0.0, pooled, 1.0)
     coef = jnp.log(pooled / lens_f)
     other = jnp.concatenate([coef[PAIRS:], coef[:PAIRS]], axis=0)
     row_of = lax.broadcasted_iota(jnp.int32, (8, prompts), 0)
@@ -282,16 +307,6 @@
         for k in range(1, XY)
     ]
 
-    c2[-1].wait_recv()
-    tile = half[-1][0, bits[-1]].astype(F32) + half_recv[-1][0].astype(F32)
-    c_blk = join3(nn(split3(jnp.exp(tile * inv)), members[...]))
-    mine = jnp.where(f == tiles, loss_part, c_blk)
-    c5_all[xy] = mine
-    c5 = [
-        remote(c5_all.at[xy], c5_all.at[xy], c5_ss.at[k], c5_rs.at[k], xy_dev(xy_peer(k)))
-        for k in range(1, XY)
-    ]
-
     c_rows = lax.broadcasted_iota(jnp.int32, (16, toks), 0)
     slope_hi = slope.astype(BF16).astype(F32)
     slope_lo = slope - slope_hi
@@ -307,6 +322,16 @@
         cp.start()
         outs.append(cp)
 
+    c2[-1].wait_recv()
+    tile = half[-1][0, bits[-1]].astype(F32) + half_recv[-1][0].astype(F32)
+    c_blk = join3(nn(split3(jnp.exp(tile * inv)), members[...]))
+    mine = jnp.where(f == tiles, loss_part, c_blk)
+    c5_all[xy] = mine
+    c5 = [
+        remote(c5_all.at[xy], c5_all.at[xy], c5_ss.at[k], c5_rs.at[k], xy_dev(xy_peer(k)))
+        for k in range(1, XY)
+    ]
+
     for cp in s4:
         cp.wait_recv()
     total = g_tile[xy]
@@ -354,21 +379,30 @@
     coef_ref[...] = table[:models]
     loss_ref[0, 0] = jnp.sum(ctab[tiles].astype(F32)[0:2, 0:1])
 
-    for cp in q_cp + i_cp + s1 + s2 + s3 + s4 + [s5] + s6 + [c1] + c2 + c5 + [c5b] + c6:
+    for cp in q_cp + i_cp + s1 + s2 + b_cp + s4 + [s5] + s6 + [c1] + c2 + c5 + [c5b] + c6:
         cp.wait_send()
     for cp in outs:
         cp.wait()
 
 
-def hand_out(loss, coef, gh, ghead, ggain, loss_o, coef_o, gh_o, ghead_o, ggain_o, sems):
-    rows = gh.shape[0] // 4
-    pairs = [(gh.at[pl.ds(n * rows, rows)], gh_o.at[pl.ds(n * rows, rows)]) for n in range(4)]
-    pairs += [(ghead, ghead_o), (coef, coef_o), (ggain, ggain_o)]
-    cps = [pltpu.make_async_copy(a, b, sems.at[n]) for n, (a, b) in enumerate(pairs)]
-    for cp in cps:
+def hand_out(
+    loss, coef, gh, ghead, ggain, loss_o, coef_o, gh_o, ghead_o, ggain_o,
+    coef_v, gh_v, ghead_v, ggain_v, sem_in, sem_out,
+):
+    rows = gh.shape[0] // 8
+    trips = [tuple([r.at[pl.ds(n * rows, rows)] for r in (gh, gh_v, gh_o)]) for n in range(8)]
+    trips += [(ghead, ghead_v, ghead_o), (coef, coef_v, coef_o), (ggain, ggain_v, ggain_o)]
+    ins, outs = [], []
+    for n, (src, mid, dst) in enumerate(trips):
+        ins.append(pltpu.make_async_copy(src, mid, sem_in.at[n]))
+        outs.append(pltpu.make_async_copy(mid, dst, sem_out.at[n]))
+    for cp in ins:
         cp.start()
     loss_o[0, 0] = loss[0, 0]
-    for cp in cps:
+    for cp_in, cp_out in zip(ins, outs):
+        cp_in.wait()
+        cp_out.start()
+    for cp in outs:
         cp.wait()
 
 
@@ -402,11 +436,11 @@
             V((toks, dl), BF16), V((1, dl), F32), V((models, dl), BF16),
             V((1, prompts), jnp.int32), V((2, n_battles), jnp.int32),
             V((wide, dl), BF16), V((wide, dl), BF16),
-            V((toks, prompts), BF16), V((2 * PAIRS, toks), F32),
+            V((toks, prompts), BF16), V((2 * PAIRS, toks), F32), V((wide, toks), F32),
             V((ZL, NC, 16, toks), BF16), V((toks, dl), BF16),
             V((F, 1, LANES), F32), V((F, 1, LANES), F32), V((F, 1, LANES), F32),
             V((F, 8, LANES), F32), V((F, 8, LANES), F32), V((F, 8, LANES), F32),
-            V((2, 8, LANES), F32), V((2, 8, LANES), F32),
+            V((1, LANES), F32), V((F, 1, LANES), F32),
             V((wide, toks), BF16), V((XY, 16, dl), F32), V((XY, 16, dl), BF16),
             V((XY, 16, dl), BF16), V((16, dl), F32), V((16, dl), F32), V((XY, 16, dl), BF16),
             V((ZL, 16, toks), BF16),
@@ -414,7 +448,7 @@
             V((F, 16, prompts), BF16),
             sem((4 + toks // blk,)), sem((toks // blk,)),
             sem((F,)), sem((F,)), sem((F,)), sem((F,)),
-            sem((F,)), sem((F,)), sem((F,)), sem((F,)), sem((2,)), sem((2,)),
+            sem((F,)), sem((F,)), sem((F,)), sem((F,)), sem((F,)), sem((F,)),
             sem((XY,)), sem((XY,)), sem, sem, sem((XY,)), sem((XY,)),
             sem, sem, sem((levels,)), sem((levels,)), sem((XY,)), sem((XY,)), sem, sem,
             sem((F,)), sem((F,)),
@@ -431,7 +465,10 @@
         out_shape=shapes,
         in_specs=[smem] + [hbm] * 4,
         out_specs=(smem,) + (hbm,) * 4,
-        scratch_shapes=[sem((7,))],
+        scratch_shapes=[
+            V((models, prompts), F32), V((toks, dl), BF16), V((models, dl), F32), V((1, dl), F32),
+            sem((11,)), sem((11,)),
+        ],
         compiler_params=pltpu.CompilerParams(vmem_limit_bytes=60 * 2**20),
         name="hand_out",
     )(*results)

time: 160 us -> 78.6 us (0.49)
  Pallas kernels: 160 us -> 77.8 us
    pallas_call x1, Pallas kernels: 84.5 us -> 3.73 us  [on_device(): pl.pallas_call(hand_out, out_shape=shapes, in_specs=[smem] + [hbm] * 4, o...]
where the time goes in v3:
time: 78.6 us; the launch traced here: 78.5 us
  Pallas kernels  77.8 us (99%)
    pallas_call x1, Pallas kernels, on_device(): pl.pallas_call(functools.partial(kernel, models, float(dl * F), float(n_b...  74.1 us
    pallas_call x1, Pallas kernels, on_device(): pl.pallas_call(hand_out, out_shape=shapes, in_specs=[smem] + [hbm] * 4, o...  3.73 us

profile of v3, /device:TPU:1, one launch (start us, length us, event | category | flops | bytes accessed | tf_op | source)
XLA Modules:
  0.0 78.5 jit_solution(9214218155781538750)
XLA Ops:
  0.6 74.1 %head.1 = (f32[1,1]{1,0:T(1,128)}, f32[200,256]{1,0:T(8,128)}, bf16[2048,512]{1,0:T(8,128)(2,1)}, f32[200,512]{1,0:T(8,128)}, f32[1,512]{1,0:T(1,128)}) custom-call(bf16[2048,512]{1,0:T(8,128)(2,1)} %hidden_hbm.1, f32[1,512]{1,0:T(1,128)} %bitcast.7, bf16[200,512]{1,0:T(8,128)(2,1)} %head_hbm.1, s32[1,256]{1,0:T(1,128)} %bitcast.8, s32[2,1024]{1,0:T(2,128)} %bitcast.6), custom_call_target="tpu_custom_call" | custom-call | tf_op jit(solution)/shard_map/head/pallas_call | solution.py:430
  74.7 3.7 %hand_out.1 = (f32[1,1]{1,0:T(1,128)}, f32[200,256]{1,0:T(8,128)}, bf16[2048,512]{1,0:T(8,128)(2,1)}, f32[200,512]{1,0:T(8,128)}, f32[1,512]{1,0:T(1,128)}) custom-call(f32[1,1]{1,0:T(1,128)} %get-tuple-element.15.loss, f32[200,256]{1,0:T(8,128)} %get-tuple-element.16.coef, bf16[2048,512]{1,0:T(8,128)(2,1)} %get-tuple-element.17.gh, ...), custom_call_target="tpu_custom_call" | custom-call | tf_op jit(solution)/shard_map/hand_out/pallas_call | solution.py:463

commit v4 on v3

--- a/solution.py
+++ b/solution.py
@@ -42,8 +42,9 @@
 def kernel(
     models, width, n_battles, blk,
     hidden_hbm, gain_hbm, head_hbm, lens_hbm, battles_hbm,
-    loss_ref, coef_ref, gh_hbm, ghead_ref, ggain_ref,
+    loss_out, coef_out, gh_out, ghead_out, ggain_out,
     hid, gain_v, head_v, lens_v, bat_v, wp, wpad, members, ids, raw, raw16, out_v,
+    loss_v, coef_v, ghead_v, ggain_v,
     q_send, q_recv, i_buf, s1_send, s1_recv, s2_buf, b_send, b_recv, g_t, g_tile, g_send, s4_recv,
     s5_send, s5_recv, ag, c1_recv, c5_all, c5_sum, c5_other, ctab,
     load_sem, out_sem, q_ss, q_rs, i_ss, i_rs, s1_ss, s1_rs, s2_ss, s2_rs, b_ss, b_rs, s4_ss, s4_rs,
@@ -130,21 +131,34 @@
         cp.start()
         return cp
 
-    for t in range(tiles, ZL * NC):
-        raw16[t // NC, t % NC] = jnp.zeros((16, toks), BF16)
+    def scatter(src, dst, ss, rs, peer, dev):
+        for k in range(1, dst.shape[0]):
+            remote(src.at[peer(k)], dst.at[k], ss, rs, dev(peer(k)))
+        rest = dst.at[pl.ds(1, dst.shape[0] - 1)]
+        return pltpu.make_async_remote_copy(
+            src_ref=rest, dst_ref=rest, send_sem=ss, recv_sem=rs, device_id=dev(peer(1)), device_id_type=MESH
+        )
+
+    def gather(buf, ss, rs, peer, dev):
+        for k in range(1, buf.shape[0]):
+            remote(buf.at[0], buf.at[k], ss, rs, dev(peer(k)))
+        rest = buf.at[pl.ds(1, buf.shape[0] - 1)]
+        return pltpu.make_async_remote_copy(
+            src_ref=rest, dst_ref=rest, send_sem=ss, recv_sem=rs, device_id=dev(peer(1)), device_id_type=MESH
+        )
+
+    def fsdp_dev(r):
+        return (dp, r)
+
+    def fsdp_slot(r):
+        return lax.rem(f + F - r, F)
+
+    def xy_slot(q):
+        return lax.rem(y + Y - q // X, Y) * X + lax.rem(x + X - q % X, X)
+
+    ones_l = jnp.ones((8, LANES), BF16)
     for i in range(n_blk):
         loads[4 + i].wait()
-        rows = pl.ds(i * blk, blk)
-        block = nt(wp[...], hid[rows, :])
-        raw[:, rows] = block
-        for t in range(tiles):
-            raw16[t // NC, t % NC, :, rows] = block[16 * t : 16 * t + 16].astype(BF16)
-
-    pl.semaphore_wait(barrier, len(partners))
-    c1 = remote(raw16.at[:, 1 - c], c1_recv, c1_ss, c1_rs, (dp, zl * NC + (1 - c)))
-
-    ones_l = jnp.ones((8, LANES), BF16)
-    for i in range(n_blk):
         hf = hid[pl.ds(i * blk, blk), :].astype(F32)
         sq = hf * hf
         part = sq[:, :LANES]
@@ -155,10 +169,19 @@
         sumsq = nt(ones_l, part_hi) + nt(ones_l, part_lo)
         for b in range(blk // LANES):
             q_send[i * (blk // LANES) + b] = sumsq[0:1, b * LANES : (b + 1) * LANES]
-    q_cp = [
-        remote(q_send.at[fsdp_peer(k)], q_recv.at[k], q_ss.at[k], q_rs.at[k], (dp, fsdp_peer(k)))
-        for k in range(1, F)
-    ]
+    pl.semaphore_wait(barrier, len(partners))
+    q_cp = scatter(q_send, q_recv, q_ss, q_rs, fsdp_peer, fsdp_dev)
+
+    for t in range(tiles, ZL * NC):
+        raw16[t // NC, t % NC] = jnp.zeros((16, toks), BF16)
+    for i in range(n_blk):
+        rows = pl.ds(i * blk, blk)
+        block = nt(wp[...], hid[rows, :])
+        raw[:, rows] = block
+        for t in range(tiles):
+            raw16[t // NC, t % NC, :, rows] = block[16 * t : 16 * t + 16].astype(BF16)
+
+    c1 = remote(raw16.at[:, 1 - c], c1_recv, c1_ss, c1_rs, (dp, zl * NC + (1 - c)))
 
     bits = [(zl >> n) % 2 for n in range(levels)]
 
@@ -171,11 +194,6 @@
         for j in range(half_recv[n].shape[0]):
             total = half[n][j, bits[n]].astype(F32) + half_recv[n][j].astype(F32)
             half[n + 1][j // 2, j % 2] = total.astype(BF16)
-
-    c1.wait_recv()
-    for k in range(ZL):
-        half[0][k // 2, k % 2] = (raw16[k, c].astype(F32) + c1_recv[k].astype(F32)).astype(BF16)
-    c2 = [halve(0)]
 
     for i in range(n_blk):
         pos = base + i * blk + lax.broadcasted_iota(jnp.int32, (blk, prompts), 0)
@@ -192,6 +210,11 @@
     bat = nn(bat.astype(F32).astype(BF16), judged.astype(F32).astype(BF16))
     ids[...] = nt(bat.astype(BF16), members[...])
 
+    c1.wait_recv()
+    for k in range(ZL):
+        half[0][k // 2, k % 2] = (raw16[k, c].astype(F32) + c1_recv[k].astype(F32)).astype(BF16)
+    c2 = [halve(0)]
+
     model_of = lax.broadcasted_iota(jnp.int32, (wide, LANES), 0).astype(F32)
     for b in range(toks // LANES):
         lanes = slice(b * LANES, (b + 1) * LANES)
@@ -203,33 +226,23 @@
         ]
         s1_send[b] = jnp.concatenate(picked, axis=0)
 
-    s1 = [
-        remote(s1_send.at[fsdp_peer(k)], s1_recv.at[k], s1_ss.at[k], s1_rs.at[k], (dp, fsdp_peer(k)))
-        for k in range(1, F)
-    ]
-    for cp in q_cp:
-        cp.wait_recv()
+    s1 = scatter(s1_send, s1_recv, s1_ss, s1_rs, fsdp_peer, fsdp_dev)
+
+    q_cp.wait_recv()
     acc = q_send[f]
     for k in range(1, F):
         acc = acc + q_recv[k]
     inv_own = lax.rsqrt(acc / width + EPS)
-    i_buf[f] = inv_own
-    i_cp = [
-        remote(i_buf.at[f], i_buf.at[f], i_ss.at[k], i_rs.at[k], (dp, fsdp_peer(k)))
-        for k in range(1, F)
-    ]
-
-    for cp in s1:
-        cp.wait_recv()
+    i_buf[0] = inv_own
+    i_cp = gather(i_buf, i_ss, i_rs, fsdp_peer, fsdp_dev)
+
+    s1.wait_recv()
     acc = s1_send[f]
     for k in range(1, F):
         acc = acc + s1_recv[k]
     own = acc * inv_own
-    s2_buf[f] = own
-    s2 = [
-        remote(s2_buf.at[f], s2_buf.at[f], s2_ss.at[k], s2_rs.at[k], (dp, fsdp_peer(k)))
-        for k in range(1, F)
-    ]
+    s2_buf[0] = own
+    s2 = gather(s2_buf, s2_ss, s2_rs, fsdp_peer, fsdp_dev)
     late = f >= F // 2
     pos = base + f * LANES + lax.broadcasted_iota(jnp.int32, (8, LANES), 1)
     pos = pos.astype(F32)
@@ -238,29 +251,29 @@
     eye = lax.broadcasted_iota(jnp.int32, (8, LANES), 0) == lax.broadcasted_iota(jnp.int32, (8, LANES), 1)
     b_send[...] = jnp.sum(jnp.where(eye, column, 0.0), axis=0, keepdims=True)
     to_dp = jnp.where(late, dp_next, dp_prev)
-    b_cp = [
-        remote(b_send, b_recv.at[f], b_ss.at[k], b_rs.at[f], (to_dp, lax.rem(f + k, F)))
-        for k in range(F)
-    ]
-
-    def b_arrival(r):
-        return pltpu.make_async_remote_copy(
-            src_ref=b_send, dst_ref=b_recv.at[r], send_sem=b_ss.at[r], recv_sem=b_rs.at[r],
-            device_id=(to_dp, f), device_id_type=MESH,
-        )
+    for k in range(F):
+        remote(b_send, b_recv.at[f], b_ss, b_rs, (to_dp, lax.rem(f + k, F)))
+    b_cp = pltpu.make_async_remote_copy(
+        src_ref=b_recv, dst_ref=b_recv, send_sem=b_ss, recv_sem=b_rs,
+        device_id=(to_dp, f), device_id_type=MESH,
+    )
 
     c2[0].wait_recv()
     fold(0)
     c2.append(halve(1))
 
-    for cp in i_cp + s2:
-        cp.wait_recv()
-    logits = jnp.concatenate([s2_buf[r] for r in range(F)], axis=1)
-    inv = jnp.concatenate([i_buf[r] for r in range(F)], axis=1)
+    for n in range(1, levels - 1):
+        c2[n].wait_recv()
+        fold(n)
+        c2.append(halve(n + 1))
+
+    i_cp.wait_recv()
+    inv = jnp.concatenate([i_buf[fsdp_slot(r)] for r in range(F)], axis=1)
+    s2.wait_recv()
+    logits = jnp.concatenate([s2_buf[fsdp_slot(r)] for r in range(F)], axis=1)
     exps = jnp.exp(logits)
     pooled = join3(nn(split3(exps), members[...]))
-    for r in range(F):
-        b_arrival(r).wait_recv()
+    b_cp.wait_recv()
 
     def column_of(rs):
         row = b_recv[rs[0]]
@@ -272,10 +285,6 @@
     from_next = column_of(range(F // 2))
     pooled = pooled + from_prev * at_prev + from_next * at_next
     pooled = jnp.where(pooled > 0.0, pooled, 1.0)
-    for n in range(1, levels - 1):
-        c2[n].wait_recv()
-        fold(n)
-        c2.append(halve(n + 1))
     coef = jnp.log(pooled / lens_f)
     other = jnp.concatenate([coef[PAIRS:], coef[:PAIRS]], axis=0)
     row_of = lax.broadcasted_iota(jnp.int32, (8, prompts), 0)
@@ -302,10 +311,14 @@
     for t in range(tiles, XY):
         g_tile[t] = jnp.zeros((16, dl), F32)
         g_send[t] = jnp.zeros((16, dl), BF16)
-    s4 = [
-        remote(g_send.at[xy_peer(k)], s4_recv.at[k], s4_ss.at[k], s4_rs.at[k], xy_dev(xy_peer(k)))
-        for k in range(1, XY)
-    ]
+    s4 = scatter(g_send, s4_recv, s4_ss, s4_rs, xy_peer, xy_dev)
+
+    c2[-1].wait_recv()
+    tile = half[-1][0, bits[-1]].astype(F32) + half_recv[-1][0].astype(F32)
+    c_blk = join3(nn(split3(jnp.exp(tile * inv)), members[...]))
+    mine = jnp.where(f == tiles, loss_part, c_blk)
+    c5_all[0] = mine
+    c5 = gather(c5_all, c5_ss, c5_rs, xy_peer, xy_dev)
 
     c_rows = lax.broadcasted_iota(jnp.int32, (16, toks), 0)
     slope_hi = slope.astype(BF16).astype(F32)
@@ -318,42 +331,27 @@
         gn = tn(g_t[:, rows], wpad[...])
         cb = tn(slope3[:, i * blk : (i + 1) * blk], ones_w)
         out_v[rows, :] = (gain_v[...] * gn - hid[rows, :].astype(F32) * cb).astype(BF16)
-        cp = pltpu.make_async_copy(out_v.at[rows], gh_hbm.at[rows], out_sem.at[i])
+        cp = pltpu.make_async_copy(out_v.at[rows], gh_out.at[rows], out_sem.at[i])
         cp.start()
         outs.append(cp)
 
-    c2[-1].wait_recv()
-    tile = half[-1][0, bits[-1]].astype(F32) + half_recv[-1][0].astype(F32)
-    c_blk = join3(nn(split3(jnp.exp(tile * inv)), members[...]))
-    mine = jnp.where(f == tiles, loss_part, c_blk)
-    c5_all[xy] = mine
-    c5 = [
-        remote(c5_all.at[xy], c5_all.at[xy], c5_ss.at[k], c5_rs.at[k], xy_dev(xy_peer(k)))
-        for k in range(1, XY)
-    ]
-
-    for cp in s4:
-        cp.wait_recv()
+    s4.wait_recv()
     total = g_tile[xy]
     for k in range(1, XY):
         total = total + s4_recv[k].astype(F32)
     s5_send[...] = total
     s5 = remote(s5_send, s5_recv, s5_ss, s5_rs, zh_dev)
 
-    for cp in c5:
-        cp.wait_recv()
-    csum = c5_all[0]
+    c5.wait_recv()
+    csum = c5_all[xy_slot(0)]
     for q in range(1, XY):
-        csum = csum + c5_all[q]
+        csum = csum + c5_all[xy_slot(q)]
     c5_sum[...] = csum
     c5b = remote(c5_sum, c5_other, c5b_ss, c5b_rs, zh_dev)
 
     s5.wait_recv()
-    ag[xy] = (s5_send[...] + s5_recv[...]).astype(BF16)
-    s6 = [
-        remote(ag.at[xy], ag.at[xy], s6_ss.at[k], s6_rs.at[k], xy_dev(xy_peer(k)))
-        for k in range(1, XY)
-    ]
+    ag[0] = (s5_send[...] + s5_recv[...]).astype(BF16)
+    s6 = gather(ag, s6_ss, s6_rs, xy_peer, xy_dev)
 
     c5b.wait_recv()
     csum = c5_sum[...] + c5_other[...]
@@ -361,48 +359,42 @@
     crow = lax.broadcasted_iota(jnp.int32, (16, prompts), 0)
     loss_blk = jnp.where(crow == 0, loss_hi, jnp.where(crow == 1, csum - loss_hi, 0.0))
     coef_blk = jnp.log(csum / lens_f)
-    ctab[f] = jnp.where(f == tiles, loss_blk, coef_blk).astype(BF16)
-    c6 = [
-        remote(ctab.at[f], ctab.at[f], c6_ss.at[k], c6_rs.at[k], (dp, fsdp_peer(k)))
-        for k in range(1, F)
-    ]
-
-    for cp in s6:
-        cp.wait_recv()
-    whole = jnp.concatenate([ag[t].astype(F32) for t in range(tiles)], axis=0)
-    ghead_ref[...] = (gain_v[...] * whole)[:models]
-    ggain_ref[...] = jnp.sum(wpad[...].astype(F32) * whole, axis=0, keepdims=True)
-
-    for cp in c6:
-        cp.wait_recv()
-    table = jnp.concatenate([ctab[t].astype(F32) for t in range(tiles)], axis=0)
-    coef_ref[...] = table[:models]
-    loss_ref[0, 0] = jnp.sum(ctab[tiles].astype(F32)[0:2, 0:1])
-
-    for cp in q_cp + i_cp + s1 + s2 + b_cp + s4 + [s5] + s6 + [c1] + c2 + c5 + [c5b] + c6:
+    ctab[0] = jnp.where(f == tiles, loss_blk, coef_blk).astype(BF16)
+    c6 = gather(ctab, c6_ss, c6_rs, fsdp_peer, fsdp_dev)
+
+    def hand(n, src, dst):
+        cp = pltpu.make_async_copy(src, dst, out_sem.at[n_blk + n])
+        cp.start()
+        outs.append(cp)
+
+    s6.wait_recv()
+    whole = jnp.concatenate([ag[xy_slot(t)].astype(F32) for t in range(tiles)], axis=0)
+    ghead_v[...] = (gain_v[...] * whole)[:models]
+    ggain_v[...] = jnp.sum(wpad[...].astype(F32) * whole, axis=0, keepdims=True)
+    hand(0, ghead_v, ghead_out)
+    hand(1, ggain_v, ggain_out)
+
+    c6.wait_recv()
+    table = jnp.concatenate([ctab[fsdp_slot(t)].astype(F32) for t in range(tiles)], axis=0)
+    coef_v[...] = table[:models]
+    loss_v[...] = jnp.sum(ctab[fsdp_slot(tiles)].astype(F32)[0:2, 0:1], axis=0, keepdims=True)
+    hand(2, coef_v, coef_out)
+    hand(3, loss_v, loss_out)
+
+    for cp in [q_cp, i_cp, s1, s2, b_cp, s4, s5, s6, c1] + c2 + [c5, c5b, c6]:
         cp.wait_send()
     for cp in outs:
         cp.wait()
 
 
-def hand_out(
-    loss, coef, gh, ghead, ggain, loss_o, coef_o, gh_o, ghead_o, ggain_o,
-    coef_v, gh_v, ghead_v, ggain_v, sem_in, sem_out,
-):
-    rows = gh.shape[0] // 8
-    trips = [tuple([r.at[pl.ds(n * rows, rows)] for r in (gh, gh_v, gh_o)]) for n in range(8)]
-    trips += [(ghead, ghead_v, ghead_o), (coef, coef_v, coef_o), (ggain, ggain_v, ggain_o)]
-    ins, outs = [], []
-    for n, (src, mid, dst) in enumerate(trips):
-        ins.append(pltpu.make_async_copy(src, mid, sem_in.at[n]))
-        outs.append(pltpu.make_async_copy(mid, dst, sem_out.at[n]))
-    for cp in ins:
+def hand_out(loss, coef, gh, ghead, ggain, loss_o, coef_o, gh_o, ghead_o, ggain_o, sems):
+    rows = gh.shape[0] // 4
+    pairs = [(gh.at[pl.ds(n * rows, rows)], gh_o.at[pl.ds(n * rows, rows)]) for n in range(4)]
+    pairs += [(ghead, ghead_o), (coef, coef_o), (ggain, ggain_o), (loss, loss_o)]
+    cps = [pltpu.make_async_copy(a, b, sems.at[n]) for n, (a, b) in enumerate(pairs)]
+    for cp in cps:
         cp.start()
-    loss_o[0, 0] = loss[0, 0]
-    for cp_in, cp_out in zip(ins, outs):
-        cp_in.wait()
-        cp_out.start()
-    for cp in outs:
+    for cp in cps:
         cp.wait()
 
 
@@ -416,28 +408,25 @@
     blk = min(512, toks)
     levels = ZL.bit_length() - 1
     sem = pltpu.SemaphoreType.DMA
-    vmem = pl.BlockSpec(memory_space=pltpu.VMEM)
-    smem = pl.BlockSpec(memory_space=pltpu.SMEM)
     hbm = pl.BlockSpec(memory_space=pl.ANY)
     V = pltpu.VMEM
-    shapes = (
-        jax.ShapeDtypeStruct((1, 1), F32),
-        jax.ShapeDtypeStruct((models, prompts), F32),
-        jax.ShapeDtypeStruct((toks, dl), BF16),
-        jax.ShapeDtypeStruct((models, dl), F32),
-        jax.ShapeDtypeStruct((1, dl), F32),
+    kinds = (
+        ((1, 1), F32), ((models, prompts), F32), ((toks, dl), BF16), ((models, dl), F32), ((1, dl), F32)
     )
+    operands = [hidden, gain.reshape(1, dl), head_weight, lengths.reshape(1, prompts), battles.T]
+    operands = [pltpu.with_memory_space_constraint(a, pltpu.HBM) for a in operands]
     results = pl.pallas_call(
         functools.partial(kernel, models, float(dl * F), float(n_battles), blk),
-        out_shape=shapes,
+        out_shape=tuple(pltpu.VMEM(*k) for k in kinds),
         in_specs=[hbm] * 5,
-        out_specs=(smem, vmem, hbm, vmem, vmem),
+        out_specs=(hbm,) * 5,
         scratch_shapes=[
             V((toks, dl), BF16), V((1, dl), F32), V((models, dl), BF16),
             V((1, prompts), jnp.int32), V((2, n_battles), jnp.int32),
             V((wide, dl), BF16), V((wide, dl), BF16),
             V((toks, prompts), BF16), V((2 * PAIRS, toks), F32), V((wide, toks), F32),
             V((ZL, NC, 16, toks), BF16), V((toks, dl), BF16),
+            V((1, 1), F32), V((models, prompts), F32), V((models, dl), F32), V((1, dl), F32),
             V((F, 1, LANES), F32), V((F, 1, LANES), F32), V((F, 1, LANES), F32),
             V((F, 8, LANES), F32), V((F, 8, LANES), F32), V((F, 8, LANES), F32),
             V((1, LANES), F32), V((F, 1, LANES), F32),
@@ -446,30 +435,22 @@
             V((ZL, 16, toks), BF16),
             V((XY, 16, prompts), F32), V((16, prompts), F32), V((16, prompts), F32),
             V((F, 16, prompts), BF16),
-            sem((4 + toks // blk,)), sem((toks // blk,)),
-            sem((F,)), sem((F,)), sem((F,)), sem((F,)),
-            sem((F,)), sem((F,)), sem((F,)), sem((F,)), sem((F,)), sem((F,)),
-            sem((XY,)), sem((XY,)), sem, sem, sem((XY,)), sem((XY,)),
-            sem, sem, sem((levels,)), sem((levels,)), sem((XY,)), sem((XY,)), sem, sem,
-            sem((F,)), sem((F,)),
+            sem((4 + toks // blk,)), sem((4 + toks // blk,)),
+            *[sem] * 18, sem((levels,)), sem((levels,)), *[sem] * 6,
         ]
         + [V((ZL >> (n + 1), 2, 16, toks), BF16) for n in range(levels)]
         + [V((ZL >> (n + 1), 16, toks), BF16) for n in range(levels)],
         compiler_params=pltpu.CompilerParams(
-            collective_id=0, has_side_effects=True, vmem_limit_bytes=60 * 2**20
+            collective_id=0, has_side_effects=True, vmem_limit_bytes=48 * 2**20
         ),
         name="head",
-    )(hidden, gain.reshape(1, dl), head_weight, lengths.reshape(1, prompts), battles.T)
+    )(*operands)
     loss, coef, gh, ghead, ggain = pl.pallas_call(
         hand_out,
-        out_shape=shapes,
-        in_specs=[smem] + [hbm] * 4,
-        out_specs=(smem,) + (hbm,) * 4,
-        scratch_shapes=[
-            V((models, prompts), F32), V((toks, dl), BF16), V((models, dl), F32), V((1, dl), F32),
-            sem((11,)), sem((11,)),
-        ],
-        compiler_params=pltpu.CompilerParams(vmem_limit_bytes=60 * 2**20),
+        out_shape=tuple(pltpu.HBM(*k) for k in kinds),
+        in_specs=[hbm] * 5,
+        out_specs=(hbm,) * 5,
+        scratch_shapes=[sem((8,))],
         name="hand_out",
     )(*results)
     return loss.reshape(()), coef.T, gh, ghead, ggain.reshape(dl)

time: 78.6 us -> 160 us (2.04)
  Pallas kernels: 77.8 us -> 156 us
  local copies, waits for them, and re-layouts: 0 us -> 3.35 us
    pallas_call x1, Pallas kernels: 3.73 us -> 83.9 us  [on_device(): pl.pallas_call(hand_out, out_shape=tuple((pltpu.HBM(*k) for k in kinds)),...]
    unnamed x0 -> x8, local copies, waits for them, and re-layouts: none -> 3.35 us
    pallas_call x1, Pallas kernels: 74.1 us -> 71.7 us  [on_device(): pl.pallas_call(functools.partial(kernel, models, float(dl * F), float(n_b...]
where the time goes in v4:
time: 160 us
  Pallas kernels  156 us (98%)
  local copies, waits for them, and re-layouts  3.35 us (2%)
    pallas_call x1, Pallas kernels, on_device(): pl.pallas_call(hand_out, out_shape=tuple((pltpu.HBM(*k) for k in kinds)),...  83.9 us
    pallas_call x1, Pallas kernels, on_device(): pl.pallas_call(functools.partial(kernel, models, float(dl * F), float(n_b...  71.7 us
    unnamed x8, local copies, waits for them, and re-layouts  3.35 us

profile of v4, /device:TPU:1, one launch (start us, length us, event | category | flops | bytes accessed | tf_op | source)
XLA Modules:
  0.0 159.6 jit_solution(14840118468557665893)
XLA Ops:
  0.6 71.7 %head.1 = (f32[1,1]{1,0:T(1,128)}, f32[200,256]{1,0:T(8,128)S(1)}, bf16[2048,512]{1,0:T(8,128)(2,1)S(1)}, f32[200,512]{1,0:T(8,128)S(1)}, f32[1,512]{1,0:T(1,128)S(1)}) custom-call(bf16[2048,512]{1,0:T(8,128)(2,1)} %hidden_hbm.1, f32[1,512]{1,0:T(1,128)} %bitcast.7, bf16[200,512]{1,0:T(8,128)(2,1)} %head_hbm.1, s32[1,256]{1,0:T(1,128)} %bitcast.8, ...), custom_call_target="tpu_custom_call" | custom-call | tf_op jit(solution)/shard_map/head/pallas_call | solution.py:418
  72.3 0.0 copy-start
  72.3 1.3 copy-done
  73.6 0.0 copy-start.1
  73.6 0.8 copy-done.1
  74.4 0.0 copy-start.2
  74.4 0.7 copy-done.2
  75.1 0.0 copy-start.3
  75.1 0.6 copy-done.3
  75.7 83.9 %hand_out.1 = (f32[1,1]{1,0:T(1,128)}, f32[200,256]{1,0:T(8,128)}, bf16[2048,512]{1,0:T(8,128)(2,1)}, f32[200,512]{1,0:T(8,128)}, f32[1,512]{1,0:T(1,128)}) custom-call(f32[1,1]{1,0:T(1,128)} %get-tuple-element.15.loss, f32[200,256]{1,0:T(8,128)} %copy-done.2, bf16[2048,512]{1,0:T(8,128)(2,1)} %copy-done, f32[200,512]{1,0:T(8,128)} %copy-done.1, ...), custom_call_target="tpu_custom_call" | custom-call | tf_op jit(solution)/shard_map/hand_out/pallas_call | solution.py:448
Async XLA Ops:
  72.3 1.3 copy-start
  73.6 0.8 copy-start.1
  74.4 0.7 copy-start.2
  75.1 0.6 copy-start.3

commit v5 on v4

--- a/solution.py
+++ b/solution.py
@@ -156,31 +156,17 @@
     def xy_slot(q):
         return lax.rem(y + Y - q // X, Y) * X + lax.rem(x + X - q % X, X)
 
-    ones_l = jnp.ones((8, LANES), BF16)
-    for i in range(n_blk):
-        loads[4 + i].wait()
-        hf = hid[pl.ds(i * blk, blk), :].astype(F32)
-        sq = hf * hf
-        part = sq[:, :LANES]
-        for j in range(1, dl // LANES):
-            part = part + sq[:, j * LANES : (j + 1) * LANES]
-        part_hi = part.astype(BF16)
-        part_lo = (part - part_hi.astype(F32)).astype(BF16)
-        sumsq = nt(ones_l, part_hi) + nt(ones_l, part_lo)
-        for b in range(blk // LANES):
-            q_send[i * (blk // LANES) + b] = sumsq[0:1, b * LANES : (b + 1) * LANES]
-    pl.semaphore_wait(barrier, len(partners))
-    q_cp = scatter(q_send, q_recv, q_ss, q_rs, fsdp_peer, fsdp_dev)
-
     for t in range(tiles, ZL * NC):
         raw16[t // NC, t % NC] = jnp.zeros((16, toks), BF16)
     for i in range(n_blk):
+        loads[4 + i].wait()
         rows = pl.ds(i * blk, blk)
         block = nt(wp[...], hid[rows, :])
         raw[:, rows] = block
         for t in range(tiles):
             raw16[t // NC, t % NC, :, rows] = block[16 * t : 16 * t + 16].astype(BF16)
 
+    pl.semaphore_wait(barrier, len(partners))
     c1 = remote(raw16.at[:, 1 - c], c1_recv, c1_ss, c1_rs, (dp, zl * NC + (1 - c)))
 
     bits = [(zl >> n) % 2 for n in range(levels)]
@@ -210,11 +196,6 @@
     bat = nn(bat.astype(F32).astype(BF16), judged.astype(F32).astype(BF16))
     ids[...] = nt(bat.astype(BF16), members[...])
 
-    c1.wait_recv()
-    for k in range(ZL):
-        half[0][k // 2, k % 2] = (raw16[k, c].astype(F32) + c1_recv[k].astype(F32)).astype(BF16)
-    c2 = [halve(0)]
-
     model_of = lax.broadcasted_iota(jnp.int32, (wide, LANES), 0).astype(F32)
     for b in range(toks // LANES):
         lanes = slice(b * LANES, (b + 1) * LANES)
@@ -227,6 +208,25 @@
         s1_send[b] = jnp.concatenate(picked, axis=0)
 
     s1 = scatter(s1_send, s1_recv, s1_ss, s1_rs, fsdp_peer, fsdp_dev)
+
+    ones_l = jnp.ones((8, LANES), BF16)
+    for i in range(n_blk):
+        hf = hid[pl.ds(i * blk, blk), :].astype(F32)
+        sq = hf * hf
+        part = sq[:, :LANES]
+        for j in range(1, dl // LANES):
+            part = part + sq[:, j * LANES : (j + 1) * LANES]
+        part_hi = part.astype(BF16)
+        part_lo = (part - part_hi.astype(F32)).astype(BF16)
+        sumsq = nt(ones_l, part_hi) + nt(ones_l, part_lo)
+        for b in range(blk // LANES):
+            q_send[i * (blk // LANES) + b] = sumsq[0:1, b * LANES : (b + 1) * LANES]
+    q_cp = scatter(q_send, q_recv, q_ss, q_rs, fsdp_peer, fsdp_dev)
+
+    c1.wait_recv()
+    for k in range(ZL):
+        half[0][k // 2, k % 2] = (raw16[k, c].astype(F32) + c1_recv[k].astype(F32)).astype(BF16)
+    c2 = [halve(0)]
 
     q_cp.wait_recv()
     acc = q_send[f]
@@ -451,8 +451,9 @@
         in_specs=[hbm] * 5,
         out_specs=(hbm,) * 5,
         scratch_shapes=[sem((8,))],
+        compiler_params=pltpu.CompilerParams(vmem_limit_bytes=2**20),
         name="hand_out",
-    )(*results)
+    )(*[pltpu.with_memory_space_constraint(a, pltpu.VMEM) for a in results])
     return loss.reshape(()), coef.T, gh, ghead, ggain.reshape(dl)
 
 

time: 160 us -> 70 us (0.44)
  Pallas kernels: 156 us -> 69.2 us
  local copies, waits for them, and re-layouts: 3.35 us -> 0 us
    pallas_call x1, Pallas kernels: 83.9 us -> 2.21 us  [on_device(): pl.pallas_call(hand_out, out_shape=tuple((pltpu.HBM(*k) for k in kinds)),...]
    pallas_call x1, Pallas kernels: 71.7 us -> 67 us  [on_device(): pl.pallas_call(functools.partial(kernel, models, float(dl * F), float(n_b...]
    unnamed x8 -> x0, local copies, waits for them, and re-layouts: 3.35 us -> none
where the time goes in v5:
time: 70 us; the launch traced here: 69.9 us
  Pallas kernels  69.2 us (99%)
    pallas_call x1, Pallas kernels, on_device(): pl.pallas_call(functools.partial(kernel, models, float(dl * F), float(n_b...  67 us
    pallas_call x1, Pallas kernels, on_device(): pl.pallas_call(hand_out, out_shape=tuple((pltpu.HBM(*k) for k in kinds)),...  2.21 us

profile of v5, /device:TPU:1, one launch (start us, length us, event | category | flops | bytes accessed | tf_op | source)
XLA Modules:
  0.0 69.9 jit_solution(8770581569859310398)
XLA Ops:
  0.6 67.0 %head.1 = (f32[1,1]{1,0:T(1,128)}, f32[200,256]{1,0:T(8,128)S(1)}, bf16[2048,512]{1,0:T(8,128)(2,1)S(1)}, f32[200,512]{1,0:T(8,128)S(1)}, f32[1,512]{1,0:T(1,128)S(1)}) custom-call(bf16[2048,512]{1,0:T(8,128)(2,1)} %hidden_hbm.1, f32[1,512]{1,0:T(1,128)} %bitcast.7, bf16[200,512]{1,0:T(8,128)(2,1)} %head_hbm.1, s32[1,256]{1,0:T(1,128)} %bitcast.8, ...), custom_call_target="tpu_custom_call" | custom-call | tf_op jit(solution)/shard_map/head/pallas_call | solution.py:418
  67.7 2.2 %hand_out.1 = (f32[1,1]{1,0:T(1,128)}, f32[200,256]{1,0:T(8,128)}, bf16[2048,512]{1,0:T(8,128)(2,1)}, f32[200,512]{1,0:T(8,128)}, f32[1,512]{1,0:T(1,128)}) custom-call(f32[1,1]{1,0:T(1,128)} %get-tuple-element.15.loss, f32[200,256]{1,0:T(8,128)S(1)} %get-tuple-element.16.coef, bf16[2048,512]{1,0:T(8,128)(2,1)S(1)} %get-tuple-element.17.gh, ...), custom_call_target="tpu_custom_call" | custom-call | tf_op jit(solution)/shard_map/hand_out/pallas_call | solution.py:448

commit v6 on v5

--- a/solution.py
+++ b/solution.py
@@ -8,7 +8,7 @@
 from jax.sharding import PartitionSpec as P
 
 Y, X, ZH, ZL, NC = 4, 4, 2, 8, 2
-XY, F, DP = Y * X, ZL * NC, Y * X * ZH
+XY, F, DP, RING = Y * X, ZL * NC, Y * X * ZH, ZH * ZL
 LANES = 128
 PAIRS = 4
 EPS = 1e-06
@@ -45,10 +45,13 @@
     loss_out, coef_out, gh_out, ghead_out, ggain_out,
     hid, gain_v, head_v, lens_v, bat_v, wp, wpad, members, ids, raw, raw16, out_v,
     loss_v, coef_v, ghead_v, ggain_v,
-    q_send, q_recv, i_buf, s1_send, s1_recv, s2_buf, b_send, b_recv, g_t, g_tile, g_send, s4_recv,
-    s5_send, s5_recv, ag, c1_recv, c5_all, c5_sum, c5_other, ctab,
-    load_sem, out_sem, q_ss, q_rs, i_ss, i_rs, s1_ss, s1_rs, s2_ss, s2_rs, b_ss, b_rs, s4_ss, s4_rs,
-    s5_ss, s5_rs, s6_ss, s6_rs, c1_ss, c1_rs, c2_ss, c2_rs, c5_ss, c5_rs, c5b_ss, c5b_rs, c6_ss, c6_rs, *halves,
+    q_send, q_core, q_pair, q_recv, i_all, s1_send, s1_core, s1_pair, s1_recv, s2_all,
+    b_send, b_core, b_sum, b_recv, g_t, g_tile, g_send, s4_recv,
+    s5_send, s5_recv, ag, c1_recv, c5_all, ctab,
+    load_sem, out_sem, qc_ss, qc_rs, q_ss, q_rs, i_ss, i_rs, ic_ss, ic_rs,
+    s1c_ss, s1c_rs, s1_ss, s1_rs, s2_ss, s2_rs, s2c_ss, s2c_rs, bc_ss, bc_rs, b_ss, b_rs, s4_ss, s4_rs,
+    s5_ss, s5_rs, s6_ss, s6_rs, c1_ss, c1_rs, c2_ss, c2_rs, c5_ss, c5_rs, c6_ss, c6_rs, c6c_ss, c6c_rs,
+    *halves,
 ):
     toks, dl = hid.shape
     prompts = members.shape[1]
@@ -62,8 +65,17 @@
     zl, c = f // NC, f % NC
     base = dp * toks
 
-    def fsdp_peer(k):
-        return lax.rem(f + k, F)
+    def ring_peer(k):
+        return lax.rem(zh * ZL + zl + k, RING)
+
+    def ring_dev(r):
+        return (xy * ZH + r // ZL, (r % ZL) * NC + c)
+
+    def ring_slot(r):
+        return lax.rem(zh * ZL + zl + RING - r, RING)
+
+    def z_peer(k):
+        return lax.rem(zl + k, ZL)
 
     def xy_peer(k):
         return lax.rem(y + k // X, Y) * X + lax.rem(x + k % X, X)
@@ -71,6 +83,7 @@
     def xy_dev(q):
         return (q * ZH + zh, f)
 
+    core_dev = (dp, zl * NC + (1 - c))
     zh_dev = (xy * ZH + (1 - zh), f)
     dp_next, dp_prev = lax.rem(dp + 1, DP), lax.rem(dp + DP - 1, DP)
 
@@ -88,10 +101,10 @@
         cp.start()
 
     barrier = pltpu.get_barrier_semaphore()
-    partners = [(dp, fsdp_peer(k)) for k in range(1, F)]
+    partners = [core_dev] + [(dp, z_peer(k) * NC + c) for k in range(1, ZL)]
     partners += [xy_dev(xy_peer(k)) for k in range(1, XY)]
-    partners += [zh_dev]
-    partners += [(dp_prev if r >= F // 2 else dp_next, r) for r in range(F)]
+    partners += [((xy * ZH + (1 - zh)), r * NC + c) for r in range(ZL)]
+    partners += [(dp_prev if r >= ZL // 2 else dp_next, r * NC + c) for r in range(ZL)]
     for dev in partners:
         pl.semaphore_signal(barrier, inc=1, device_id=dev, device_id_type=MESH)
 
@@ -110,6 +123,11 @@
     lens_f = lens.astype(F32)
     at_prev = ((starts < base) & (ends > base)).astype(F32)
     at_next = ((starts < base + toks) & (ends > base + toks)).astype(F32)
+    here = jnp.minimum(ends, base + toks) - jnp.maximum(starts, base)
+    here = jnp.maximum(here, 0).astype(F32)
+    first, last = starts // toks, (ends - 1) // toks
+    in_first = jnp.where(first == last, lens, last * toks - starts)
+    in_low = jnp.where(first % ZH == 0, in_first, lens - in_first)
     owned = ((ends > base) & (ends <= base + toks)).astype(F32)
     before_end = jnp.sum(at_prev * ends.astype(F32), axis=1, keepdims=True)
     from_start = jnp.sum(at_next * starts.astype(F32), axis=1, keepdims=True)
@@ -147,11 +165,11 @@
             src_ref=rest, dst_ref=rest, send_sem=ss, recv_sem=rs, device_id=dev(peer(1)), device_id_type=MESH
         )
 
-    def fsdp_dev(r):
-        return (dp, r)
-
-    def fsdp_slot(r):
-        return lax.rem(f + F - r, F)
+    def z_dev(r):
+        return (dp, r * NC + c)
+
+    def z_slot(r):
+        return lax.rem(zl + ZL - r, ZL)
 
     def xy_slot(q):
         return lax.rem(y + Y - q // X, Y) * X + lax.rem(x + X - q % X, X)
@@ -196,19 +214,6 @@
     bat = nn(bat.astype(F32).astype(BF16), judged.astype(F32).astype(BF16))
     ids[...] = nt(bat.astype(BF16), members[...])
 
-    model_of = lax.broadcasted_iota(jnp.int32, (wide, LANES), 0).astype(F32)
-    for b in range(toks // LANES):
-        lanes = slice(b * LANES, (b + 1) * LANES)
-        block = raw[:, lanes]
-        id_blk = ids[:, lanes]
-        picked = [
-            jnp.sum(jnp.where(model_of == id_blk[j : j + 1], block, 0.0), axis=0, keepdims=True)
-            for j in range(2 * PAIRS)
-        ]
-        s1_send[b] = jnp.concatenate(picked, axis=0)
-
-    s1 = scatter(s1_send, s1_recv, s1_ss, s1_rs, fsdp_peer, fsdp_dev)
-
     ones_l = jnp.ones((8, LANES), BF16)
     for i in range(n_blk):
         hf = hid[pl.ds(i * blk, blk), :].astype(F32)
@@ -220,29 +225,50 @@
         part_lo = (part - part_hi.astype(F32)).astype(BF16)
         sumsq = nt(ones_l, part_hi) + nt(ones_l, part_lo)
         for b in range(blk // LANES):
-            q_send[i * (blk // LANES) + b] = sumsq[0:1, b * LANES : (b + 1) * LANES]
-    q_cp = scatter(q_send, q_recv, q_ss, q_rs, fsdp_peer, fsdp_dev)
-
+            dest = i * (blk // LANES) + b
+            q_send[dest % NC, dest // NC] = sumsq[0:1, b * LANES : (b + 1) * LANES]
+    qc = remote(q_send.at[1 - c], q_core, qc_ss, qc_rs, core_dev)
+
+    model_of = lax.broadcasted_iota(jnp.int32, (wide, LANES), 0).astype(F32)
+    for b in range(toks // LANES):
+        lanes = slice(b * LANES, (b + 1) * LANES)
+        id_blk = ids[:, lanes]
+        found = [jnp.zeros((8, LANES), F32) for _ in range(2 * PAIRS)]
+        for t in range(wide // 8):
+            rows = slice(8 * t, 8 * t + 8)
+            block, number = raw[rows, lanes], model_of[rows]
+            found = [jnp.where(number == id_blk[j : j + 1], block, found[j]) for j in range(2 * PAIRS)]
+        picked = [jnp.sum(one, axis=0, keepdims=True) for one in found]
+        s1_send[b % NC, b // NC] = jnp.concatenate(picked, axis=0)
+
+    s1c = remote(s1_send.at[1 - c], s1_core, s1c_ss, s1c_rs, core_dev)
+    qc.wait_recv()
+    q_pair[...] = q_send[c] + q_core[...]
+    q_cp = scatter(q_pair, q_recv, q_ss, q_rs, z_peer, z_dev)
     c1.wait_recv()
     for k in range(ZL):
         half[0][k // 2, k % 2] = (raw16[k, c].astype(F32) + c1_recv[k].astype(F32)).astype(BF16)
+    s1c.wait_recv()
+    s1_pair[...] = s1_send[c] + s1_core[...]
+    s1 = scatter(s1_pair, s1_recv, s1_ss, s1_rs, z_peer, z_dev)
     c2 = [halve(0)]
 
+
     q_cp.wait_recv()
-    acc = q_send[f]
-    for k in range(1, F):
+    acc = q_pair[zl]
+    for k in range(1, ZL):
         acc = acc + q_recv[k]
     inv_own = lax.rsqrt(acc / width + EPS)
-    i_buf[0] = inv_own
-    i_cp = gather(i_buf, i_ss, i_rs, fsdp_peer, fsdp_dev)
-
+    i_all[c, 0] = inv_own
     s1.wait_recv()
-    acc = s1_send[f]
-    for k in range(1, F):
+    acc = s1_pair[zl]
+    for k in range(1, ZL):
         acc = acc + s1_recv[k]
     own = acc * inv_own
-    s2_buf[0] = own
-    s2 = gather(s2_buf, s2_ss, s2_rs, fsdp_peer, fsdp_dev)
+    s2_all[c, 0] = own
+    s2 = gather(s2_all.at[c], s2_ss, s2_rs, z_peer, z_dev)
+    i_cp = gather(i_all.at[c], i_ss, i_rs, z_peer, z_dev)
+
     late = f >= F // 2
     pos = base + f * LANES + lax.broadcasted_iota(jnp.int32, (8, LANES), 1)
     pos = pos.astype(F32)
@@ -251,8 +277,11 @@
     eye = lax.broadcasted_iota(jnp.int32, (8, LANES), 0) == lax.broadcasted_iota(jnp.int32, (8, LANES), 1)
     b_send[...] = jnp.sum(jnp.where(eye, column, 0.0), axis=0, keepdims=True)
     to_dp = jnp.where(late, dp_next, dp_prev)
-    for k in range(F):
-        remote(b_send, b_recv.at[f], b_ss, b_rs, (to_dp, lax.rem(f + k, F)))
+    bc = remote(b_send, b_core, bc_ss, bc_rs, core_dev)
+    bc.wait_recv()
+    b_sum[...] = b_send[...] + b_core[...]
+    for k in range(ZL):
+        remote(b_sum, b_recv.at[zl], b_ss, b_rs, (to_dp, z_peer(k) * NC + c))
     b_cp = pltpu.make_async_remote_copy(
         src_ref=b_recv, dst_ref=b_recv, send_sem=b_ss, recv_sem=b_rs,
         device_id=(to_dp, f), device_id_type=MESH,
@@ -262,15 +291,19 @@
     fold(0)
     c2.append(halve(1))
 
+    s2.wait_recv()
+    s2c = remote(s2_all.at[c], s2_all.at[c], s2c_ss, s2c_rs, core_dev)
+    i_cp.wait_recv()
+    ic = remote(i_all.at[c], i_all.at[c], ic_ss, ic_rs, core_dev)
     for n in range(1, levels - 1):
         c2[n].wait_recv()
         fold(n)
         c2.append(halve(n + 1))
 
-    i_cp.wait_recv()
-    inv = jnp.concatenate([i_buf[fsdp_slot(r)] for r in range(F)], axis=1)
-    s2.wait_recv()
-    logits = jnp.concatenate([s2_buf[fsdp_slot(r)] for r in range(F)], axis=1)
+    s2c.wait_recv()
+    ic.wait_recv()
+    logits = jnp.concatenate([s2_all[r % NC, z_slot(r // NC)] for r in range(F)], axis=1)
+    inv = jnp.concatenate([i_all[r % NC, z_slot(r // NC)] for r in range(F)], axis=1)
     exps = jnp.exp(logits)
     pooled = join3(nn(split3(exps), members[...]))
     b_cp.wait_recv()
@@ -281,8 +314,8 @@
             row = row + b_recv[r]
         return jnp.sum(jnp.where(eye, row, 0.0), axis=1, keepdims=True)
 
-    from_prev = column_of(range(F // 2, F))
-    from_next = column_of(range(F // 2))
+    from_prev = column_of(range(ZL // 2, ZL))
+    from_next = column_of(range(ZL // 2))
     pooled = pooled + from_prev * at_prev + from_next * at_next
     pooled = jnp.where(pooled > 0.0, pooled, 1.0)
     coef = jnp.log(pooled / lens_f)
@@ -300,10 +333,16 @@
     for b in range(toks // LANES):
         lanes = slice(b * LANES, (b + 1) * LANES)
         id_blk = ids[:, lanes]
-        full = jnp.zeros((wide, LANES), F32)
+        g_blk = grads[:, lanes]
+        same = jnp.zeros((8, LANES), F32)
         for j in range(2 * PAIRS):
-            full = full + jnp.where(model_of == id_blk[j : j + 1], grads[j : j + 1, lanes], 0.0)
-        g_t[:, lanes] = full.astype(BF16)
+            same = same + jnp.where(id_blk == id_blk[j : j + 1], g_blk[j : j + 1], 0.0)
+        for t in range(wide // 16):
+            rows = slice(16 * t, 16 * t + 16)
+            full = jnp.zeros((16, LANES), F32)
+            for j in range(2 * PAIRS):
+                full = jnp.where(model_of[rows] == id_blk[j : j + 1], same[j : j + 1], full)
+            g_t[rows, lanes] = full.astype(BF16)
     head_part = nn(g_t[...], hid[...])
     for t in range(tiles):
         g_tile[t] = head_part[16 * t : 16 * t + 16]
@@ -316,9 +355,33 @@
     c2[-1].wait_recv()
     tile = half[-1][0, bits[-1]].astype(F32) + half_recv[-1][0].astype(F32)
     c_blk = join3(nn(split3(jnp.exp(tile * inv)), members[...]))
-    mine = jnp.where(f == tiles, loss_part, c_blk)
+    local = jnp.log(jnp.where(here > 0.0, c_blk, 1.0) / jnp.maximum(here, 1.0))
+    crow = lax.broadcasted_iota(jnp.int32, (16, prompts), 0)
+
+    def loss_rows(total):
+        hi = total.astype(BF16).astype(F32)
+        mid = (total - hi).astype(BF16).astype(F32)
+        return jnp.where(crow == 0, hi, jnp.where(crow == 1, mid, jnp.where(crow == 2, total - hi - mid, 0.0)))
+
+    loss_part = jnp.broadcast_to(loss_part, (16, prompts))
+    mine = jnp.where(f == tiles, loss_rows(loss_part), local).astype(BF16)
     c5_all[0] = mine
     c5 = gather(c5_all, c5_ss, c5_rs, xy_peer, xy_dev)
+
+    s4.wait_recv()
+    total = g_tile[xy]
+    for k in range(1, XY):
+        total = total + s4_recv[k].astype(F32)
+    s5_send[...] = total
+    s5 = remote(s5_send, s5_recv, s5_ss, s5_rs, zh_dev)
+
+    c5.wait_recv()
+    csum = c5_all[xy_slot(0)].astype(F32)
+    for q in range(1, XY):
+        csum = csum + c5_all[xy_slot(q)].astype(F32)
+    csum = jnp.where(f == tiles, loss_rows(csum[0:1] + csum[1:2] + csum[2:3]), csum)
+    ctab[c, 0] = csum.astype(BF16)
+    c6 = gather(ctab.at[c], c6_ss, c6_rs, ring_peer, ring_dev)
 
     c_rows = lax.broadcasted_iota(jnp.int32, (16, toks), 0)
     slope_hi = slope.astype(BF16).astype(F32)
@@ -335,38 +398,17 @@
         cp.start()
         outs.append(cp)
 
-    s4.wait_recv()
-    total = g_tile[xy]
-    for k in range(1, XY):
-        total = total + s4_recv[k].astype(F32)
-    s5_send[...] = total
-    s5 = remote(s5_send, s5_recv, s5_ss, s5_rs, zh_dev)
-
-    c5.wait_recv()
-    csum = c5_all[xy_slot(0)]
-    for q in range(1, XY):
-        csum = csum + c5_all[xy_slot(q)]
-    c5_sum[...] = csum
-    c5b = remote(c5_sum, c5_other, c5b_ss, c5b_rs, zh_dev)
-
     s5.wait_recv()
     ag[0] = (s5_send[...] + s5_recv[...]).astype(BF16)
     s6 = gather(ag, s6_ss, s6_rs, xy_peer, xy_dev)
-
-    c5b.wait_recv()
-    csum = c5_sum[...] + c5_other[...]
-    loss_hi = csum.astype(BF16).astype(F32)
-    crow = lax.broadcasted_iota(jnp.int32, (16, prompts), 0)
-    loss_blk = jnp.where(crow == 0, loss_hi, jnp.where(crow == 1, csum - loss_hi, 0.0))
-    coef_blk = jnp.log(csum / lens_f)
-    ctab[0] = jnp.where(f == tiles, loss_blk, coef_blk).astype(BF16)
-    c6 = gather(ctab, c6_ss, c6_rs, fsdp_peer, fsdp_dev)
 
     def hand(n, src, dst):
         cp = pltpu.make_async_copy(src, dst, out_sem.at[n_blk + n])
         cp.start()
         outs.append(cp)
 
+    c6.wait_recv()
+    c6c = remote(ctab.at[c], ctab.at[c], c6c_ss, c6c_rs, core_dev)
     s6.wait_recv()
     whole = jnp.concatenate([ag[xy_slot(t)].astype(F32) for t in range(tiles)], axis=0)
     ghead_v[...] = (gain_v[...] * whole)[:models]
@@ -374,14 +416,23 @@
     hand(0, ghead_v, ghead_out)
     hand(1, ggain_v, ggain_out)
 
-    c6.wait_recv()
-    table = jnp.concatenate([ctab[fsdp_slot(t)].astype(F32) for t in range(tiles)], axis=0)
+    c6c.wait_recv()
+
+    def slot_of(half_at, t):
+        return ctab[t % NC, ring_slot(half_at * ZL + t // NC)].astype(F32)
+
+    low, high = (jnp.concatenate([slot_of(n, t) for t in range(tiles)], axis=0) for n in range(ZH))
+    low_share = in_low.astype(F32) / lens_f
+    high_share = (lens - in_low).astype(F32) / lens_f
+    table = jnp.log(low_share * jnp.exp(low) + high_share * jnp.exp(high))
+    table = jnp.where(in_low == lens, low, jnp.where(in_low == 0, high, table))
     coef_v[...] = table[:models]
-    loss_v[...] = jnp.sum(ctab[fsdp_slot(tiles)].astype(F32)[0:2, 0:1], axis=0, keepdims=True)
+    loss_all = slot_of(0, tiles) + slot_of(1, tiles)
+    loss_v[...] = jnp.sum(loss_all[0:3, 0:1], axis=0, keepdims=True)
     hand(2, coef_v, coef_out)
     hand(3, loss_v, loss_out)
 
-    for cp in [q_cp, i_cp, s1, s2, b_cp, s4, s5, s6, c1] + c2 + [c5, c5b, c6]:
+    for cp in [qc, q_cp, i_cp, ic, s1c, s1, s2, s2c, bc, b_cp, s4, s5, s6, c1] + c2 + [c5, c6, c6c]:
         cp.wait_send()
     for cp in outs:
         cp.wait()
@@ -427,16 +478,15 @@
             V((toks, prompts), BF16), V((2 * PAIRS, toks), F32), V((wide, toks), F32),
             V((ZL, NC, 16, toks), BF16), V((toks, dl), BF16),
             V((1, 1), F32), V((models, prompts), F32), V((models, dl), F32), V((1, dl), F32),
-            V((F, 1, LANES), F32), V((F, 1, LANES), F32), V((F, 1, LANES), F32),
-            V((F, 8, LANES), F32), V((F, 8, LANES), F32), V((F, 8, LANES), F32),
-            V((1, LANES), F32), V((F, 1, LANES), F32),
+            V((NC, ZL, 1, LANES), F32), *[V((ZL, 1, LANES), F32)] * 3, V((NC, ZL, 1, LANES), F32),
+            V((NC, ZL, 8, LANES), F32), *[V((ZL, 8, LANES), F32)] * 3, V((NC, ZL, 8, LANES), F32),
+            *[V((1, LANES), F32)] * 3, V((ZL, 1, LANES), F32),
             V((wide, toks), BF16), V((XY, 16, dl), F32), V((XY, 16, dl), BF16),
             V((XY, 16, dl), BF16), V((16, dl), F32), V((16, dl), F32), V((XY, 16, dl), BF16),
             V((ZL, 16, toks), BF16),
-            V((XY, 16, prompts), F32), V((16, prompts), F32), V((16, prompts), F32),
-            V((F, 16, prompts), BF16),
+            V((XY, 16, prompts), BF16), V((NC, RING, 16, prompts), BF16),
             sem((4 + toks // blk,)), sem((4 + toks // blk,)),
-            *[sem] * 18, sem((levels,)), sem((levels,)), *[sem] * 6,
+            *[sem] * 28, sem((levels,)), sem((levels,)), *[sem] * 6,
         ]
         + [V((ZL >> (n + 1), 2, 16, toks), BF16) for n in range(levels)]
         + [V((ZL >> (n + 1), 16, toks), BF16) for n in range(levels)],

time: 70 us -> 66.2 us (0.946)
  Pallas kernels: 69.2 us -> 65 us
    pallas_call x1, Pallas kernels: 67 us -> 62.8 us  [on_device(): pl.pallas_call(functools.partial(kernel, models, float(dl * F), float(n_b...]
where the time goes in v6:
time: 66.2 us; the launch traced here: 65.7 us
  Pallas kernels  65 us (98%)
    pallas_call x1, Pallas kernels, on_device(): pl.pallas_call(functools.partial(kernel, models, float(dl * F), float(n_b...  62.8 us
    pallas_call x1, Pallas kernels, on_device(): pl.pallas_call(hand_out, out_shape=tuple((pltpu.HBM(*k) for k in kinds)),...  2.21 us

profile of v6, /device:TPU:1, one launch (start us, length us, event | category | flops | bytes accessed | tf_op | source)
XLA Modules:
  0.0 65.7 jit_solution(8578334046026093941)
XLA Ops:
  0.6 62.8 %head.1 = (f32[1,1]{1,0:T(1,128)}, f32[200,256]{1,0:T(8,128)S(1)}, bf16[2048,512]{1,0:T(8,128)(2,1)S(1)}, f32[200,512]{1,0:T(8,128)S(1)}, f32[1,512]{1,0:T(1,128)S(1)}) custom-call(bf16[2048,512]{1,0:T(8,128)(2,1)} %hidden_hbm.1, f32[1,512]{1,0:T(1,128)} %bitcast.7, bf16[200,512]{1,0:T(8,128)(2,1)} %head_hbm.1, s32[1,256]{1,0:T(1,128)} %bitcast.8, ...), custom_call_target="tpu_custom_call" | custom-call | tf_op jit(solution)/shard_map/head/pallas_call | solution.py:469
  63.5 2.2 %hand_out.1 = (f32[1,1]{1,0:T(1,128)}, f32[200,256]{1,0:T(8,128)}, bf16[2048,512]{1,0:T(8,128)(2,1)}, f32[200,512]{1,0:T(8,128)}, f32[1,512]{1,0:T(1,128)}) custom-call(f32[1,1]{1,0:T(1,128)} %get-tuple-element.15.loss, f32[200,256]{1,0:T(8,128)S(1)} %get-tuple-element.16.coef, bf16[2048,512]{1,0:T(8,128)(2,1)S(1)} %get-tuple-element.17.gh, ...), custom_call_target="tpu_custom_call" | custom-call | tf_op jit(solution)/shard_map/hand_out/pallas_call | solution.py:498

commit v7 on v6

--- a/solution.py
+++ b/solution.py
@@ -87,6 +87,14 @@
     zh_dev = (xy * ZH + (1 - zh), f)
     dp_next, dp_prev = lax.rem(dp + 1, DP), lax.rem(dp + DP - 1, DP)
 
+    barrier = pltpu.get_barrier_semaphore()
+    partners = [core_dev] + [(dp, z_peer(k) * NC + c) for k in range(1, ZL)]
+    partners += [xy_dev(xy_peer(k)) for k in range(1, XY)]
+    partners += [((xy * ZH + (1 - zh)), r * NC + c) for r in range(ZL)]
+    partners += [(dp_prev if r >= ZL // 2 else dp_next, r * NC + c) for r in range(ZL)]
+    for dev in partners[::-1]:
+        pl.semaphore_signal(barrier, inc=1, device_id=dev, device_id_type=MESH)
+
     loads = [
         pltpu.make_async_copy(lens_hbm, lens_v, load_sem.at[0]),
         pltpu.make_async_copy(battles_hbm, bat_v, load_sem.at[1]),
@@ -99,14 +107,6 @@
         loads.append(pltpu.make_async_copy(hidden_hbm.at[rows], hid.at[rows], load_sem.at[4 + i]))
     for cp in loads:
         cp.start()
-
-    barrier = pltpu.get_barrier_semaphore()
-    partners = [core_dev] + [(dp, z_peer(k) * NC + c) for k in range(1, ZL)]
-    partners += [xy_dev(xy_peer(k)) for k in range(1, XY)]
-    partners += [((xy * ZH + (1 - zh)), r * NC + c) for r in range(ZL)]
-    partners += [(dp_prev if r >= ZL // 2 else dp_next, r * NC + c) for r in range(ZL)]
-    for dev in partners:
-        pl.semaphore_signal(barrier, inc=1, device_id=dev, device_id_type=MESH)
 
     loads[0].wait()
     lens = jnp.broadcast_to(lens_v[...], (8, prompts))
@@ -184,9 +184,6 @@
         for t in range(tiles):
             raw16[t // NC, t % NC, :, rows] = block[16 * t : 16 * t + 16].astype(BF16)
 
-    pl.semaphore_wait(barrier, len(partners))
-    c1 = remote(raw16.at[:, 1 - c], c1_recv, c1_ss, c1_rs, (dp, zl * NC + (1 - c)))
-
     bits = [(zl >> n) % 2 for n in range(levels)]
 
     def halve(n):
@@ -227,8 +224,6 @@
         for b in range(blk // LANES):
             dest = i * (blk // LANES) + b
             q_send[dest % NC, dest // NC] = sumsq[0:1, b * LANES : (b + 1) * LANES]
-    qc = remote(q_send.at[1 - c], q_core, qc_ss, qc_rs, core_dev)
-
     model_of = lax.broadcasted_iota(jnp.int32, (wide, LANES), 0).astype(F32)
     for b in range(toks // LANES):
         lanes = slice(b * LANES, (b + 1) * LANES)
@@ -241,16 +236,20 @@
         picked = [jnp.sum(one, axis=0, keepdims=True) for one in found]
         s1_send[b % NC, b // NC] = jnp.concatenate(picked, axis=0)
 
+    pl.semaphore_wait(barrier, len(partners))
     s1c = remote(s1_send.at[1 - c], s1_core, s1c_ss, s1c_rs, core_dev)
+    qc = remote(q_send.at[1 - c], q_core, qc_ss, qc_rs, core_dev)
+    c1 = remote(raw16.at[:, 1 - c], c1_recv, c1_ss, c1_rs, (dp, zl * NC + (1 - c)))
+
+    s1c.wait_recv()
+    s1_pair[...] = s1_send[c] + s1_core[...]
+    s1 = scatter(s1_pair, s1_recv, s1_ss, s1_rs, z_peer, z_dev)
     qc.wait_recv()
     q_pair[...] = q_send[c] + q_core[...]
     q_cp = scatter(q_pair, q_recv, q_ss, q_rs, z_peer, z_dev)
     c1.wait_recv()
     for k in range(ZL):
         half[0][k // 2, k % 2] = (raw16[k, c].astype(F32) + c1_recv[k].astype(F32)).astype(BF16)
-    s1c.wait_recv()
-    s1_pair[...] = s1_send[c] + s1_core[...]
-    s1 = scatter(s1_pair, s1_recv, s1_ss, s1_rs, z_peer, z_dev)
     c2 = [halve(0)]
 
 

time: 66.2 us -> 65 us (0.982)
  the two profiles are of different devices: /device:TPU:1 before, /device:TPU:32 now
where the time goes in v7:
time: 65 us; the launch traced here: 64.9 us
  Pallas kernels  64.2 us (99%)
    pallas_call x1, Pallas kernels, on_device(): pl.pallas_call(functools.partial(kernel, models, float(dl * F), float(n_b...  62 us
    pallas_call x1, Pallas kernels, on_device(): pl.pallas_call(hand_out, out_shape=tuple((pltpu.HBM(*k) for k in kinds)),...  2.21 us

profile of v7, /device:TPU:32, one launch (start us, length us, event | category | flops | bytes accessed | tf_op | source)
XLA Modules:
  0.0 64.9 jit_solution(17911328605532738427)
XLA Ops:
  0.6 62.0 %head.1 = (f32[1,1]{1,0:T(1,128)}, f32[200,256]{1,0:T(8,128)S(1)}, bf16[2048,512]{1,0:T(8,128)(2,1)S(1)}, f32[200,512]{1,0:T(8,128)S(1)}, f32[1,512]{1,0:T(1,128)S(1)}) custom-call(bf16[2048,512]{1,0:T(8,128)(2,1)} %hidden_hbm.1, f32[1,512]{1,0:T(1,128)} %bitcast.7, bf16[200,512]{1,0:T(8,128)(2,1)} %head_hbm.1, s32[1,256]{1,0:T(1,128)} %bitcast.8, ...), custom_call_target="tpu_custom_call" | custom-call | tf_op jit(solution)/shard_map/head/pallas_call | solution.py:468
  62.7 2.2 %hand_out.1 = (f32[1,1]{1,0:T(1,128)}, f32[200,256]{1,0:T(8,128)}, bf16[2048,512]{1,0:T(8,128)(2,1)}, f32[200,512]{1,0:T(8,128)}, f32[1,512]{1,0:T(1,128)}) custom-call(f32[1,1]{1,0:T(1,128)} %get-tuple-element.15.loss, f32[200,256]{1,0:T(8,128)S(1)} %get-tuple-element.16.coef, bf16[2048,512]{1,0:T(8,128)(2,1)S(1)} %get-tuple-element.17.gh, ...), custom_call_target="tpu_custom_call" | custom-call | tf_op jit(solution)/shard_map/hand_out/pallas_call | solution.py:497

commit v8 on v7

--- a/solution.py
+++ b/solution.py
@@ -322,12 +322,11 @@
     row_of = lax.broadcasted_iota(jnp.int32, (8, prompts), 0)
     sign = jnp.where(row_of < PAIRS, -1.0, 1.0)
     margin = sign * (coef - other)
-    softplus = jnp.maximum(margin, 0.0) + jnp.log1p(jnp.exp(-jnp.abs(margin)))
-    loss_part = jnp.sum(jnp.where(row_of < PAIRS, softplus * owned, 0.0)) / n_battles
     ratio = sign * (1.0 / (1.0 + jnp.exp(-margin))) / n_battles / pooled
     grads = exps * join3(nt(split3(ratio), members[...]))
     slope = jnp.sum(grads * logits, axis=0, keepdims=True) * inv * inv / width
     grads = grads * inv
+    model_16 = model_of.astype(BF16)
 
     for b in range(toks // LANES):
         lanes = slice(b * LANES, (b + 1) * LANES)
@@ -336,12 +335,14 @@
         same = jnp.zeros((8, LANES), F32)
         for j in range(2 * PAIRS):
             same = same + jnp.where(id_blk == id_blk[j : j + 1], g_blk[j : j + 1], 0.0)
+        one_id = [jnp.broadcast_to(id_blk[j : j + 1], (16, LANES)).astype(BF16) for j in range(2 * PAIRS)]
+        one_g = [jnp.broadcast_to(same[j : j + 1], (16, LANES)).astype(BF16) for j in range(2 * PAIRS)]
         for t in range(wide // 16):
             rows = slice(16 * t, 16 * t + 16)
-            full = jnp.zeros((16, LANES), F32)
+            full = jnp.zeros((16, LANES), BF16)
             for j in range(2 * PAIRS):
-                full = jnp.where(model_of[rows] == id_blk[j : j + 1], same[j : j + 1], full)
-            g_t[rows, lanes] = full.astype(BF16)
+                full = jnp.where(model_16[rows] == one_id[j], one_g[j], full)
+            g_t[rows, lanes] = full
     head_part = nn(g_t[...], hid[...])
     for t in range(tiles):
         g_tile[t] = head_part[16 * t : 16 * t + 16]
@@ -350,6 +351,9 @@
         g_tile[t] = jnp.zeros((16, dl), F32)
         g_send[t] = jnp.zeros((16, dl), BF16)
     s4 = scatter(g_send, s4_recv, s4_ss, s4_rs, xy_peer, xy_dev)
+
+    softplus = jnp.maximum(margin, 0.0) + jnp.log1p(jnp.exp(-jnp.abs(margin)))
+    loss_part = jnp.sum(jnp.where(row_of < PAIRS, softplus * owned, 0.0)) / n_battles
 
     c2[-1].wait_recv()
     tile = half[-1][0, bits[-1]].astype(F32) + half_recv[-1][0].astype(F32)

time: 65 us -> 64.8 us (level)
  no operation moved by 1% of the time
where the time goes in v8:
time: 64.8 us; the launch traced here: 64.6 us
  Pallas kernels  64 us (99%)
    pallas_call x1, Pallas kernels, on_device(): pl.pallas_call(functools.partial(kernel, models, float(dl * F), float(n_b...  61.8 us
    pallas_call x1, Pallas kernels, on_device(): pl.pallas_call(hand_out, out_shape=tuple((pltpu.HBM(*k) for k in kinds)),...  2.21 us

profile of v8, /device:TPU:32, one launch (start us, length us, event | category | flops | bytes accessed | tf_op | source)
XLA Modules:
  0.0 64.6 jit_solution(17082243153811121434)
XLA Ops:
  0.6 61.8 %head.1 = (f32[1,1]{1,0:T(1,128)}, f32[200,256]{1,0:T(8,128)S(1)}, bf16[2048,512]{1,0:T(8,128)(2,1)S(1)}, f32[200,512]{1,0:T(8,128)S(1)}, f32[1,512]{1,0:T(1,128)S(1)}) custom-call(bf16[2048,512]{1,0:T(8,128)(2,1)} %hidden_hbm.1, f32[1,512]{1,0:T(1,128)} %bitcast.7, bf16[200,512]{1,0:T(8,128)(2,1)} %head_hbm.1, s32[1,256]{1,0:T(1,128)} %bitcast.8, ...), custom_call_target="tpu_custom_call" | custom-call | tf_op jit(solution)/shard_map/head/pallas_call | solution.py:472
  62.4 2.2 %hand_out.1 = (f32[1,1]{1,0:T(1,128)}, f32[200,256]{1,0:T(8,128)}, bf16[2048,512]{1,0:T(8,128)(2,1)}, f32[200,512]{1,0:T(8,128)}, f32[1,512]{1,0:T(1,128)}) custom-call(f32[1,1]{1,0:T(1,128)} %get-tuple-element.15.loss, f32[200,256]{1,0:T(8,128)S(1)} %get-tuple-element.16.coef, bf16[2048,512]{1,0:T(8,128)(2,1)S(1)} %get-tuple-element.17.gh, ...), custom_call_target="tpu_custom_call" | custom-call | tf_op jit(solution)/shard_map/hand_out/pallas_call | solution.py:501
